TPU v7x, 256 devices: a whole 4x4x8 slice. The times are simulated.
256 devices in a mesh: dom: 128 (over y, z, x), feat: 2 (over core).
Axes of the slice: x: 4, y: 4, z: 8, core: 2. Of those that a mesh axis runs over, the one named last changes fastest.
Arguments:
- features: bfloat16 [16384, 128], P('dom'), may hold values from -6 to 6
- w_self: bfloat16 [128, 256], P(None, 'feat'), may hold values from -0.5 to 0.5
- w_neigh: bfloat16 [128, 256], P(None, 'feat'), may hold values from -6 to 6
- tiles: bfloat16 [16384, 128, 128], P('dom'), may hold values from 0 to 1, as said below
- dest: int32 [16384, 1], P('dom'), may hold values from 0 to 127; in each aligned block of 128 rows (0 to 127, 128 to 255, ...) at most 2 rows name the same one
- outside: int32 [16384], P('dom'), may hold values from 1 to 256
- cotangent: bfloat16 [16384, 256], P('dom', 'feat'), may hold values from -6 to 6
Outputs:
- output: bfloat16 [16384, 256], P('dom', 'feat')
- grad_input: bfloat16 [16384, 128], P('dom')
- grad_self: float32 [128, 256], P(None, 'feat')
- grad_neigh: float32 [128, 256], P(None, 'feat')
Inputs may be any that keep to these rules, and one draw needn't show every extreme that they name: `dest`: among the 128 tiles of one index of dom, at most 2 name one destination block, and some block is named by exactly 2. `tiles`: entries are 0 or 1.
All inputs are finite; a program needn't handle non-finite values.
Results may differ from a plain program's by a relative error of at most 0.015.
Values may be sent and summed in bfloat16 or wider, within the bound.
A program may use at most 128 MiB of HBM per device.

v0:
```python
import jax
import jax.numpy as jnp
from jax import lax
from jax.sharding import PartitionSpec as P

CAP = 2


def on_device(features, w_self, w_neigh, tiles, dest, outside, cotangent):
    peers = lax.axis_size("dom")
    tile_count, rows, _ = tiles.shape
    hidden_local = w_self.shape[1]
    self_part = jnp.dot(features, w_self, preferred_element_type=jnp.float32)
    message = jnp.dot(features, w_neigh, preferred_element_type=jnp.float32).astype(jnp.bfloat16)
    targets = dest[:, 0]
    dest_onehot = (targets[:, None] == jnp.arange(peers, dtype=jnp.int32)[None, :]).astype(
        jnp.bfloat16
    )
    flat_tiles = tiles.reshape(tile_count, rows * rows)
    dest_tiles = jnp.einsum(
        "td,tij->idj", dest_onehot, tiles, preferred_element_type=jnp.float32
    ).astype(jnp.bfloat16)
    counts = dest_onehot.astype(jnp.int32)
    before = jnp.cumsum(counts, axis=0) - counts
    rank = jnp.sum(before * counts, axis=1)
    slot = targets * CAP + rank
    slot_onehot = (slot[None, :] == jnp.arange(peers * CAP, dtype=jnp.int32)[:, None]).astype(
        jnp.bfloat16
    )
    slot_tiles = jnp.dot(slot_onehot, flat_tiles, preferred_element_type=jnp.float32).astype(
        jnp.bfloat16
    )
    slot_tiles = slot_tiles.reshape(peers * CAP, rows, rows)
    slot_links = jnp.sum(slot_tiles.astype(jnp.float32), axis=1).reshape(peers, CAP * rows)
    partial_sums = jnp.einsum(
        "sij,ik->sjk", slot_tiles, message, preferred_element_type=jnp.float32
    )
    partial_sums = partial_sums.reshape(peers, CAP * rows, hidden_local)
    arrived, arrived_links = (
        lax.all_to_all(partial_sums, "dom", split_axis=0, concat_axis=0, tiled=True),
        lax.all_to_all(slot_links, "dom", split_axis=0, concat_axis=0, tiled=True),
    )
    summed = jnp.sum(arrived.reshape(peers * CAP, rows, hidden_local), axis=0)
    links = jnp.sum(arrived_links.reshape(peers * CAP, rows), axis=0)
    inverse = 1.0 / (links + outside.astype(jnp.float32))
    pre = self_part + summed * inverse[:, None]
    sigma = jax.nn.sigmoid(pre)
    output = (pre * sigma).astype(jnp.bfloat16)
    dpre = (cotangent.astype(jnp.float32) * sigma * (1.0 + pre * (1.0 - sigma))).astype(
        jnp.bfloat16
    )
    dagg = (dpre.astype(jnp.float32) * inverse[:, None]).astype(jnp.bfloat16)
    dest_columns = dest_tiles.reshape(rows, peers * rows)
    dmessage = jnp.dot(
        dest_columns,
        lax.all_gather(dagg, "dom", axis=0, tiled=True),
        preferred_element_type=jnp.float32,
    )
    dmessage = dmessage.astype(jnp.bfloat16)
    both_grads = jnp.concatenate([dpre, dmessage], axis=1)
    local_term = lax.dot_general(
        features, both_grads, (((0,), (0,)), ((), ())), preferred_element_type=jnp.float32
    )
    weight_sum = lax.psum(local_term, "dom")
    grad_self = weight_sum[:, :hidden_local]
    grad_neigh = weight_sum[:, hidden_local:]
    input_term = lax.dot_general(
        dpre, w_self, (((1,), (1,)), ((), ())), preferred_element_type=jnp.float32
    )
    input_term = input_term + lax.dot_general(
        dmessage, w_neigh, (((1,), (1,)), ((), ())), preferred_element_type=jnp.float32
    )
    grad_input = lax.psum(input_term, "feat").astype(jnp.bfloat16)
    return (output, grad_input, grad_self, grad_neigh)


def solution(mesh):
    placed = (
        P("dom", None),
        P(None, "feat"),
        P(None, "feat"),
        P("dom", None, None),
        P("dom", None),
        P("dom"),
        P("dom", "feat"),
    )
    return jax.shard_map(
        on_device,
        mesh=mesh,
        in_specs=placed,
        out_specs=(P("dom", "feat"), P("dom", None), P(None, "feat"), P(None, "feat")),
        check_vma=False,
    )
```

profile of v0, /device:TPU:1, one launch (start us, length us, event | category | flops | bytes accessed | tf_op | source)
XLA Modules:
  0.0 789.4 jit_solution(4982927221599288570)
XLA Ops:
  7.2 0.0 copy-start
  7.2 0.7 fusion.24
  7.9 0.2 reduce_window_sum.11
  8.1 0.8 fusion.16
  8.9 0.7 multiply_add_fusion
  9.6 8.9 %fusion = bf16[32,8,128,128]{3,1,2,0:T(8,128)(2,1)} fusion(bf16[16,8,128,128]{3,2,1,0:T(8,128)(2,1)} %bitcast.45, s32[128]{0:T(128)S(1)} %multiply_add_fusion), kind=kOutput, calls=%fused_computation.2 | convolution fusion | flops 1077968896 | bytes 12583424 | tf_op jit(solution)/shard_map/dot_general | solution.py:30
  18.5 9.2 %copy.29 = bf16[32,8,128,128]{3,2,1,0:T(8,128)(2,1)} copy(bf16[32,8,128,128]{3,1,2,0:T(8,128)(2,1)} %fusion) | data formatting | bytes 16777216
  27.7 6.8 convert_reduce_fusion
  34.5 16.3 %all-to-all-start.1 = ((f32[128,1,256]{2,1,0:T(1,128)}), f32[128,1,256]{2,1,0:T(1,128)S(1)}, u32[]{:S(2)}, u32[]{:S(2)}) async-start(f32[128,1,256]{2,1,0:T(1,128)} %bitcast.5), calls=%async_computation.1 | async-start | bytes 262144 | tf_op jit(solution)/shard_map/all_to_all | solution.py:41
  50.8 0.0 copy-start.1
  50.9 11.9 %copy.18 = bf16[256,128,128]{2,1,0:T(8,128)(2,1)} copy(bf16[256,128,128]{1,2,0:T(8,128)(2,1)} %bitcast.43) | data formatting | bytes 16777216 | tf_op jit(solution)/shard_map/sij,ik->sjk/dot_general | solution.py:35
  62.8 0.0 copy-done
  62.8 0.0 copy-done.1
  62.8 9.3 %fusion.15 = f32[128,256,128]{2,1,0:T(8,128)} fusion(bf16[128,256,128]{2,1,0:T(8,128)(2,1)} %bitcast.44, bf16[128,128]{1,0:T(8,128)(2,1)S(1)} %copy-done, bf16[128,128]{1,0:T(8,128)(2,1)S(1)} %copy-done.1), kind=kOutput, calls=%fused_computation.17 | convolution fusion | flops 1077952512 | bytes 25231360 | tf_op jit(solution)/shard_map/sij,ik->sjk/dot_general | solution.py:35
  72.1 0.0 copy-start.2
  72.1 0.0 copy-start.5
  72.1 0.0 all-to-all-done.1
  72.1 13.9 %all-to-all-start = ((f32[128,256,128]{2,1,0:T(8,128)}), f32[128,256,128]{2,1,0:T(8,128)}, u32[]{:S(2)}, u32[]{:S(2)}) async-start(f32[128,256,128]{2,1,0:T(8,128)} %fusion.15), calls=%async_computation | async-start | bytes 33554432 | tf_op jit(solution)/shard_map/all_to_all | solution.py:40
  86.0 0.0 all-gather.2.cloned.1.call-start
  86.1 0.0 copy-done.2
  86.1 0.1 copy.20
  86.2 0.1 reduce_sum.39
  86.2 0.0 copy-done.5
  86.3 363.0 %all-to-all-done = f32[128,256,128]{2,1,0:T(8,128)} async-done(((f32[128,256,128]{2,1,0:T(8,128)}), f32[128,256,128]{2,1,0:T(8,128)}, u32[]{:S(2)}, u32[]{:S(2)}) %all-to-all-start) | async-done | bytes 16777248 | tf_op jit(solution)/shard_map/all_to_all | solution.py:40
  449.3 0.0 copy-start.3
  449.3 0.0 copy-start.4
  449.3 6.6 reduce_sum.37
  455.9 0.1 copy.19
  456.0 0.0 copy-done.3
  456.0 0.9 multiply_convert_fusion
  456.9 0.0 all-gather.2.cloned.1.call-update
  456.9 0.0 all-reduce.2.cloned.1.call-start
  457.0 0.0 copy-done.4
  457.0 7.7 fusion.8
  464.6 0.7 copy.23
  465.3 0.2 fusion.28
  465.5 95.2 %all-gather.2.cloned.1.call-done = bf16[16384,128]{0,1:T(8,128)(2,1)} async-done(((bf16[128,128]{0,1:T(8,128)(2,1)}), bf16[16384,128]{0,1:T(8,128)(2,1)}) %all-gather.2.cloned.1.call-update) | async-done | bytes 4194320 | tf_op jit(solution)/shard_map/all_gather | solution.py:56
  560.7 7.9 %fusion.11 = bf16[128,128]{0,1:T(8,128)(2,1)S(1)} fusion(bf16[16384,128]{0,1:T(8,128)(2,1)} %all-gather.2.cloned.1.call-done, bf16[16,8,128,128]{3,2,1,0:T(8,128)(2,1)} %bitcast.46), kind=kOutput, calls=%fused_computation.14 | convolution fusion | flops 536887296 | bytes 8421376 | tf_op jit(solution)/shard_map/dot_general | solution.py:54
  568.6 0.8 convolution_bitcast_fusion
  569.4 0.0 all-reduce.2.cloned.1.call-update
  569.5 0.2 convolution_add_fusion
  569.7 7.9 psum.14
  577.5 202.7 %all-reduce.2.cloned.1.call-done = f32[128,256]{0,1:T(8,128)} async-done(((f32[128,256]{0,1:T(8,128)}), f32[128,256]{0,1:T(8,128)}) %all-reduce.2.cloned.1.call-update) | async-done | bytes 131088 | tf_op jit(solution)/shard_map/psum | solution.py:64
  780.2 0.9 fusion.27
  781.1 0.7 copy.24
  781.8 0.7 copy.25
  (1 shorter events, 0.0 us)
Async XLA Ops:
  7.2 55.6 %copy-start = (bf16[128,128]{1,0:T(8,128)(2,1)S(1)}, bf16[128,128]{1,0:T(8,128)(2,1)}, u32[]{:S(2)}) copy-start(bf16[128,128]{1,0:T(8,128)(2,1)} %param.7) | copy-start | bytes 98308
  34.5 37.6 %all-to-all-start.1 = ((f32[128,1,256]{2,1,0:T(1,128)}), f32[128,1,256]{2,1,0:T(1,128)S(1)}, u32[]{:S(2)}, u32[]{:S(2)}) async-start(f32[128,1,256]{2,1,0:T(1,128)} %bitcast.5), calls=%async_computation.1 | async-start | bytes 262144 | tf_op jit(solution)/shard_map/all_to_all | solution.py:41
  50.8 12.0 %copy-start.1 = (bf16[128,128]{1,0:T(8,128)(2,1)S(1)}, bf16[128,128]{1,0:T(8,128)(2,1)}, u32[]{:S(2)}) copy-start(bf16[128,128]{1,0:T(8,128)(2,1)} %param.9) | copy-start | bytes 98308
  72.1 14.0 %copy-start.2 = (bf16[128,128]{1,0:T(8,128)(2,1)S(1)}, bf16[128,128]{1,0:T(8,128)(2,1)}, u32[]{:S(2)}) copy-start(bf16[128,128]{1,0:T(8,128)(2,1)} %param.13) | copy-start | bytes 98308
  72.1 14.2 %copy-start.5 = (s32[128]{0:T(128)S(1)}, s32[128]{0:T(128)}, u32[]{:S(2)}) copy-start(s32[128]{0:T(128)} %param.12) | copy-start | bytes 1540
  72.1 377.2 %all-to-all-start = ((f32[128,256,128]{2,1,0:T(8,128)}), f32[128,256,128]{2,1,0:T(8,128)}, u32[]{:S(2)}, u32[]{:S(2)}) async-start(f32[128,256,128]{2,1,0:T(8,128)} %fusion.15), calls=%async_computation | async-start | bytes 33554432 | tf_op jit(solution)/shard_map/all_to_all | solution.py:40
  86.0 474.7 %all-gather.2.cloned.1.call-start = ((), (), s32[]{:S(2)}) async-start(), calls=%async_computation.2 | async-start | bytes 4227072 | tf_op jit(solution)/shard_map/all_gather | solution.py:56
  449.3 6.7 copy-start.3
  449.3 7.7 copy-start.4
  456.9 323.3 %all-reduce.2.cloned.1.call-start = ((), (), s32[]{:S(2)}) async-start(), calls=%async_computation.3 | async-start | bytes 262144 | tf_op jit(solution)/shard_map/psum | solution.py:64
Sparse Core Ops, SparseCore 0:
  457.0 103.6 all-gather.1
  569.6 210.5 all-reduce.1
where the time goes:
time: 794 us; the launch traced here: 789 us
  waiting for transfers between devices  661 us (83%)
  matrix products  35.7 us (4%)
  starting transfers between devices  30.3 us (4%)
  local copies, waits for them, and re-layouts  24.4 us (3%)
  other arithmetic  15.9 us (2%)
  between operations  14.2 us (2%)
    all_to_all x1, waiting for transfers between devices, on_device(): lax.all_to_all(partial_sums, 'dom', split_axis=0, concat_axis=0, tiled=True)  363 us
    psum x1, waiting for transfers between devices, on_device(): weight_sum = lax.psum(local_term, 'dom')  203 us
    all_gather x1, waiting for transfers between devices, on_device(): lax.all_gather(dagg, 'dom', axis=0, tiled=True)  95.2 us
    all_to_all x1, starting transfers between devices, on_device(): lax.all_to_all(slot_links, 'dom', split_axis=0, concat_axis=0, tiled=True)  16.3 us
  transfers between devices with their start and end apart: 4, of which 3 were waited for; matrix products, arithmetic and copies ran while one was open for 4% of the time, Pallas kernels for 0%

commit v1 on v0

v1 whole, which is shorter than its diff:
```python
import jax
import jax.numpy as jnp
from jax import lax
from jax.experimental import pallas as pl
from jax.experimental.pallas import tpu as pltpu
from jax.sharding import PartitionSpec as P

MESH = pl.DeviceIdType.MESH
BF = jnp.bfloat16
F32 = jnp.float32
NX, NY, NZ = 4, 4, 8
B = 128
SPREAD = (2, 1, 3)


def far_first(p):
    half = (p + 1) // 2
    return 4 + half * (1 - 2 * (p % 2))


def kernel(
    feat_h, ws_h, wn_h, tiles_h, dest_h, outside_h, cot_h,
    out_h, gi_h, gs_h, gn_h,
    feat, ws, wn, dest, outside, cot, out_o, gi_o,
    tiles, adj, xt, idx_v, idx_s, selfp,
    sx, sy, r1x, r1y, p1x, p1y, r2x, r2y, p2x, p2y, r3,
    lk, rlk1, plk, rlk2, lk2, rlk3,
    gpart, grecv, gx, gy,
    w0, rw1, w1, rw2, rw3, wg, gis, gir,
    load_sem, s1, rs1x, rs1y, s2, rs2, s3, rs3, sl, rsl, sg, rsg,
    sa, ra, sb, rbx, rby, sc, rcx, rcy, sw, rw, out_sem,
):
    dom = lax.axis_index("dom")
    c = lax.axis_index("feat")
    x = lax.rem(dom, NX)
    z = lax.rem(dom // NX, NZ)
    y = dom // (NX * NZ)
    oc = 1 - c

    def dev(px, py, pz, pc):
        return ((py * NZ + pz) * NX + px, pc)

    def xp(k):
        return lax.rem(x + k, NX)

    def yp(k):
        return lax.rem(y + k, NY)

    def zp(k):
        return lax.rem(z + k, NZ)

    def push(src, dst, send, recv, device):
        pltpu.make_async_remote_copy(
            src_ref=src, dst_ref=dst, send_sem=send, recv_sem=recv,
            device_id=device, device_id_type=MESH,
        ).start()

    def take(ref, sem):
        pltpu.make_async_copy(ref, ref, sem).wait()

    loads = [
        pltpu.make_async_copy(src, dst, load_sem.at[i])
        for i, (src, dst) in enumerate(
            (
                (dest_h, dest), (tiles_h, tiles.at[pl.ds(0, B)]), (feat_h, feat), (ws_h, ws),
                (wn_h, wn), (cot_h, cot), (outside_h, outside),
            )
        )
    ]
    for load in loads:
        load.start()

    barrier = pltpu.get_barrier_semaphore()
    greeted = 0
    for pc in (c, oc):
        for k in (1, 2, 3):
            for d in (dev(xp(k), y, z, pc), dev(x, yp(k), z, pc)):
                pl.semaphore_signal(barrier, inc=1, device_id=d, device_id_type=MESH)
                greeted += 1
    for k in range(1, NZ):
        pl.semaphore_signal(barrier, inc=1, device_id=dev(x, y, zp(k), c), device_id_type=MESH)
        greeted += 1
    pl.semaphore_signal(barrier, inc=1, device_id=dev(x, y, z, oc), device_id_type=MESH)
    greeted += 1

    loads[0].wait()
    named = jnp.broadcast_to(dest[...], (B, B)).T
    lanes = lax.broadcasted_iota(jnp.int32, (B, B), 1)
    rows = lax.broadcasted_iota(jnp.int32, (B, B), 0)
    hit = named == lanes
    last = jnp.max(jnp.where(hit, rows, -1), axis=0, keepdims=True)
    first = jnp.min(jnp.where(hit, rows, B), axis=0, keepdims=True)
    idx_v[0:1, :] = first
    idx_v[1:2, :] = jnp.where(last > first, last, B)
    table = pltpu.make_async_copy(idx_v, idx_s, load_sem.at[7])
    table.start()
    tiles[B] = jnp.zeros((B, B), BF)
    loads[2].wait()
    features = feat[...]
    xt[0:B, :] = features.astype(F32).T.astype(BF)
    xh = xt[pl.ds(pl.multiple_of(c * 64, 64), 64), :]
    left = jnp.concatenate([xh, jnp.ones((16, B), BF)], axis=0)
    loads[3].wait()
    selfp[...] = jnp.dot(features, ws[...], preferred_element_type=F32)
    lk[...] = jnp.zeros_like(lk)
    table.wait()
    loads[1].wait()
    pl.semaphore_wait(barrier, greeted)

    def first_phase(p, carry):
        dz = zp(far_first(p))
        for py in range(NY):
            parts = []
            for px in range(NX):
                d = (py * NZ + dz) * NX + px
                both = tiles[idx_s[0, d]] + tiles[idx_s[1, d]]
                adj[p, py, :, px * B:(px + 1) * B] = both
                parts.append(both)
            o = jnp.dot(left, jnp.concatenate(parts, axis=1), preferred_element_type=F32)
            for px in range(NX):
                part = o[:, px * B:(px + 1) * B]
                sx[p, px, py] = part[0:32].astype(BF)
                sy[p, py, px] = part[32:64].astype(BF)
                lk[px, p, py:py + 1, :] = part[64:65]
        for k in SPREAD:
            push(sx.at[p, xp(k)], r1x.at[p, k - 1], s1.at[0], rs1x.at[p], dev(xp(k), y, z, c))
            push(sy.at[p, yp(k)], r1y.at[p, k - 1], s1.at[1], rs1y.at[p], dev(x, yp(k), z, c))
        return carry

    lax.fori_loop(0, NZ, first_phase, 0)
    for k in SPREAD:
        push(lk.at[xp(k)], rlk1.at[k - 1], sl.at[0], rsl.at[0], dev(xp(k), y, z, c))

    def add_four(own, got):
        total = own.astype(F32)
        for k in range(3):
            total = total + got[k].astype(F32)
        return total

    def second_phase(p, carry):
        to = dev(x, y, zp(far_first(p)), c)
        take(r1x.at[p], rs1x.at[p])
        p1x[p] = add_four(sx[p, x], r1x.at[p]).astype(BF)
        push(p1x.at[p], r2x.at[p], s2.at[0], rs2.at[0], to)
        take(r1y.at[p], rs1y.at[p])
        p1y[p] = add_four(sy[p, y], r1y.at[p]).astype(BF)
        push(p1y.at[p], r2y.at[p], s2.at[1], rs2.at[1], to)
        return carry

    lax.fori_loop(0, NZ - 1, second_phase, 0)
    take(rlk1, rsl.at[0])
    plk[...] = lk[x] + rlk1[0] + rlk1[1] + rlk1[2]
    for p in range(NZ - 1):
        push(plk.at[p], rlk2.at[p], sl.at[1], rsl.at[1], dev(x, y, zp(far_first(p)), c))
    own = NZ - 1
    take(r1x.at[own], rs1x.at[own])
    keep_x = add_four(sx[own, x], r1x.at[own])
    take(r1y.at[own], rs1y.at[own])
    keep_y = add_four(sy[own, y], r1y.at[own])

    take(r2x, rs2.at[0])
    for p in range(NZ - 1):
        keep_x = keep_x + r2x[p].astype(F32)
    p2x[...] = keep_x.astype(BF)
    for pc in (c, oc):
        for k in SPREAD:
            push(p2x.at[yp(k)], r3.at[c * 4 + k], s3, rs3, dev(x, yp(k), z, pc))
    push(p2x.at[y], r3.at[c * 4], s3, rs3, dev(x, y, z, oc))
    take(r2y, rs2.at[1])
    for p in range(NZ - 1):
        keep_y = keep_y + r2y[p].astype(F32)
    p2y[...] = keep_y.astype(BF)
    for pc in (c, oc):
        for k in SPREAD:
            push(p2y.at[xp(k)], r3.at[8 + c * 4 + k], s3, rs3, dev(xp(k), y, z, pc))
    push(p2y.at[x], r3.at[8 + c * 4], s3, rs3, dev(x, y, z, oc))
    take(rlk2, rsl.at[1])
    total = plk[own]
    for p in range(NZ - 1):
        total = total + rlk2[p]
    lk2[...] = total
    for k in SPREAD:
        push(lk2, rlk3.at[k - 1], sl.at[2], rsl.at[2], dev(x, yp(k), z, c))
    r3[c * 4] = p2x[y]
    r3[8 + c * 4] = p2y[x]
    loads[6].wait()
    take(rlk3, rsl.at[2])
    links = lk2[pl.ds(y, 1), :]
    for k in range(3):
        links = links + rlk3[k, pl.ds(y, 1), :]
    inverse = 1.0 / (links + outside[...].astype(F32))
    take(r3.at[pl.ds(0, 14)], rs3)
    pieces = []
    for pc in range(2):
        for share in range(2):
            slot = share * 8 + pc * 4
            piece = r3[slot].astype(F32)
            for k in range(1, 4):
                piece = piece + r3[slot + k].astype(F32)
            pieces.append(piece)
    mean_t = jnp.concatenate(pieces, axis=0) * inverse
    mean_tb = mean_t.astype(BF)

    loads[4].wait()
    loads[5].wait()
    pre = selfp[...] + jnp.dot(mean_t.T.astype(BF), wn[...], preferred_element_type=F32)
    sigma = jax.nn.sigmoid(pre)
    out_o[...] = (pre * sigma).astype(BF)
    emit = [pltpu.make_async_copy(out_o, out_h, out_sem.at[0])]
    emit[0].start()
    dpre = (cot[...].astype(F32) * sigma * (1.0 + pre * (1.0 - sigma))).astype(BF)
    across = (((1,), (1,)), ((), ()))
    gpart[...] = lax.dot_general(wn[...], dpre, across, preferred_element_type=F32) * inverse
    push(gpart.at[pl.ds(pl.multiple_of(oc * 64, 64), 64)], grecv, sg.at[0], rsg.at[0], dev(x, y, z, oc))
    grad_s = jnp.dot(xt[...], dpre, preferred_element_type=F32)
    grad_n = jnp.dot(mean_tb, dpre, preferred_element_type=F32)
    for k in range(2):
        w0[k] = grad_s[64 * k:64 * k + 64]
        w0[k + 2] = grad_n[64 * k:64 * k + 64]
    direct = lax.dot_general(dpre, ws[...], across, preferred_element_type=F32)
    take(grecv, rsg.at[0])
    gfull = (gpart[pl.ds(pl.multiple_of(c * 64, 64), 64), :] + grecv[...]).astype(BF)
    gx[0, x, y] = gfull[0:32]
    gy[0, y, x] = gfull[32:64]

    for k in SPREAD:
        push(gx.at[0, x, y], gx.at[0, x, y], sa.at[0], ra.at[0], dev(x, yp(k), z, c))
        push(gy.at[0, y, x], gy.at[0, y, x], sa.at[1], ra.at[1], dev(xp(k), y, z, c))
    for k in SPREAD:
        push(w0.at[xp(k)], rw1.at[k - 1], sw.at[0], rw.at[0], dev(xp(k), y, z, c))

    near = (0, 7, 1, 6, 2, 5, 3, 4)
    take(gx.at[0, x, pl.ds(0, 3)], ra.at[0])
    for q in range(1, NZ):
        push(gx.at[0, x], gx.at[q, x], sb.at[0], rbx.at[q], dev(x, y, zp(NZ - near[q]), c))
    take(gy.at[0, y, pl.ds(0, 3)], ra.at[1])
    for q in range(1, NZ):
        push(gy.at[0, y], gy.at[q, y], sb.at[1], rby.at[q], dev(x, y, zp(NZ - near[q]), c))

    def forward(q):
        if q > 0:
            take(gx.at[q, x], rbx.at[q])
        for k in SPREAD:
            push(gx.at[q, x], gx.at[q, x], sc.at[0], rcx.at[q], dev(xp(k), y, z, c))
        if q > 0:
            take(gy.at[q, y], rby.at[q])
        for k in SPREAD:
            push(gy.at[q, y], gy.at[q, y], sc.at[1], rcy.at[q], dev(x, yp(k), z, c))

    for q in range(0, 3):
        forward(q)
    take(rw1, rw.at[0])
    w1[...] = (w0[x] + rw1[0] + rw1[1] + rw1[2]).reshape(4, 16, B)
    for k in SPREAD:
        push(w1.at[yp(k)], rw2.at[k - 1], sw.at[1], rw.at[1], dev(x, yp(k), z, c))
    for q in range(3, NZ):
        forward(q)
    take(rw2, rw.at[1])
    rw3[z] = w1[y] + rw2[0] + rw2[1] + rw2[2]
    for k in range(1, NZ):
        push(rw3.at[z], rw3.at[z], sw.at[2], rw.at[2], dev(x, y, zp(k), c))

    def last_phase(q, acc):
        take(gx.at[q, pl.ds(0, 3)], rcx.at[q])
        take(gy.at[q, pl.ds(0, 3)], rcy.at[q])
        for py in range(NY):
            right = jnp.concatenate(
                [jnp.concatenate([gx[q, px, py], gy[q, py, px]], axis=0) for px in range(NX)], axis=1
            )
            acc = acc + lax.dot_general(adj[NZ - 1 - q, py], right, across, preferred_element_type=F32)
        return acc

    acc = lax.fori_loop(0, 3, last_phase, jnp.zeros((B, 64), F32))
    take(rw3.at[pl.ds(0, 7)], rw.at[2])
    total = rw3[0]
    for k in range(1, NZ):
        total = total + rw3[k]
    wg[x, y] = total
    for k in SPREAD:
        push(wg.at[x, y], wg.at[x, y], sw.at[3], rw.at[3], dev(x, yp(k), z, c))
    acc = lax.fori_loop(3, 6, last_phase, acc)
    take(wg.at[x, pl.ds(0, 3)], rw.at[3])
    for k in SPREAD:
        push(wg.at[x], wg.at[x], sw.at[4], rw.at[4], dev(xp(k), y, z, c))
    acc = lax.fori_loop(6, 8, last_phase, acc)

    none = jnp.zeros((B, 64), F32)
    placed = jnp.where(c == 0, jnp.concatenate([acc, none], axis=1), jnp.concatenate([none, acc], axis=1))
    gis[...] = placed + direct
    push(gis, gir, sg.at[1], rsg.at[1], dev(x, y, z, oc))
    take(wg.at[pl.ds(0, 3)], rw.at[4])
    emit.append(pltpu.make_async_copy(wg.at[pl.ds(0, 2)], gs_h, out_sem.at[1]))
    emit.append(pltpu.make_async_copy(wg.at[pl.ds(2, 2)], gn_h, out_sem.at[2]))
    emit[1].start()
    emit[2].start()

    take(sx.at[:, pl.ds(0, 3)], s1.at[0])
    take(sy.at[:, pl.ds(0, 3)], s1.at[1])
    take(lk.at[pl.ds(0, 3)], sl.at[0])
    take(p1x.at[pl.ds(0, 7)], s2.at[0])
    take(p1y.at[pl.ds(0, 7)], s2.at[1])
    take(plk.at[pl.ds(0, 7)], sl.at[1])
    take(r3.at[pl.ds(0, 14)], s3)
    take(rlk3, sl.at[2])
    take(grecv, sg.at[0])
    take(gx.at[0, 0, pl.ds(0, 3)], sa.at[0])
    take(gy.at[0, 0, pl.ds(0, 3)], sa.at[1])
    take(gx.at[pl.ds(0, 7), 0], sb.at[0])
    take(gy.at[pl.ds(0, 7), 0], sb.at[1])
    take(gx.at[:, pl.ds(0, 3)], sc.at[0])
    take(gy.at[:, pl.ds(0, 3)], sc.at[1])
    take(rw1, sw.at[0])
    take(rw2, sw.at[1])
    take(rw3.at[pl.ds(0, 7)], sw.at[2])
    take(wg.at[0, pl.ds(0, 3)], sw.at[3])
    take(wg.at[pl.ds(0, 3)], sw.at[4])
    take(gir, rsg.at[1])
    gi_o[...] = (gis[...] + gir[...]).astype(BF)
    emit.append(pltpu.make_async_copy(gi_o, gi_h, out_sem.at[3]))
    emit[3].start()
    take(gis, sg.at[1])
    for copy in emit:
        copy.wait()


def hand_out(a, b, d, e, ao, bo, do, eo, sems):
    copies = [
        pltpu.make_async_copy(src, dst, sems.at[i])
        for i, (src, dst) in enumerate(((a, ao), (b, bo), (d, do), (e, eo)))
    ]
    for copy in copies:
        copy.start()
    for copy in copies:
        copy.wait()


def on_device(features, w_self, w_neigh, tiles, dest, outside, cotangent):
    hbm = pl.BlockSpec(memory_space=pltpu.HBM)
    dma = pltpu.SemaphoreType.DMA
    V = pltpu.VMEM
    results = pl.pallas_call(
        kernel,
        out_shape=(
            jax.ShapeDtypeStruct((B, B), BF),
            jax.ShapeDtypeStruct((B, B), BF),
            jax.ShapeDtypeStruct((2, NY, 16, B), F32),
            jax.ShapeDtypeStruct((2, NY, 16, B), F32),
        ),
        in_specs=[hbm] * 7,
        out_specs=(hbm,) * 4,
        scratch_shapes=[
            V((B, B), BF), V((B, B), BF), V((B, B), BF), V((1, B), jnp.int32), V((1, B), jnp.int32),
            V((B, B), BF), V((B, B), BF), V((B, B), BF),
            V((B + 1, B, B), BF),
            V((NZ, NY, B, NX * B), BF),
            V((B, B), BF),
            V((8, B), jnp.int32),
            pltpu.SMEM((8, B), jnp.int32),
            V((B, B), F32),
            V((NZ, NX, NY, 32, B), BF),
            V((NZ, NY, NX, 32, B), BF),
            V((NZ, 3, NY, 32, B), BF),
            V((NZ, 3, NX, 32, B), BF),
            V((NZ, NY, 32, B), BF),
            V((NZ, NX, 32, B), BF),
            V((NZ - 1, NY, 32, B), BF),
            V((NZ - 1, NX, 32, B), BF),
            V((NY, 32, B), BF),
            V((NX, 32, B), BF),
            V((16, 32, B), BF),
            V((NX, NZ, 8, B), F32),
            V((3, NZ, 8, B), F32),
            V((NZ, 8, B), F32),
            V((NZ - 1, 8, B), F32),
            V((8, B), F32),
            V((3, 8, B), F32),
            V((B, B), F32),
            V((64, B), F32),
            V((NZ, NX, NY, 32, B), BF),
            V((NZ, NY, NX, 32, B), BF),
            V((4, 64, B), F32),
            V((3, 64, B), F32),
            V((4, 16, B), F32),
            V((3, 16, B), F32),
            V((NZ, 16, B), F32),
            V((NX, NY, 16, B), F32),
            V((B, B), F32),
            V((B, B), F32),
            dma((8,)),
            dma((2,)), dma((NZ,)), dma((NZ,)),
            dma((2,)), dma((2,)),
            dma(()), dma(()),
            dma((3,)), dma((3,)),
            dma((2,)), dma((2,)),
            dma((2,)), dma((2,)),
            dma((2,)), dma((NZ,)), dma((NZ,)),
            dma((2,)), dma((NZ,)), dma((NZ,)),
            dma((5,)), dma((5,)),
            dma((4,)),
        ],
        compiler_params=pltpu.CompilerParams(
            collective_id=0, has_side_effects=True, vmem_limit_bytes=60 * 2**20
        ),
        name="sage",
    )(features, w_self, w_neigh, tiles, dest.reshape(1, B), outside.reshape(1, B), cotangent)
    results = pl.pallas_call(
        hand_out,
        out_shape=tuple(jax.ShapeDtypeStruct(r.shape, r.dtype) for r in results),
        in_specs=[hbm] * 4,
        out_specs=(hbm,) * 4,
        scratch_shapes=[dma((4,))],
        name="hand_out",
    )(*results)
    output, grad_input, grad_self, grad_neigh = results
    return output, grad_input, grad_self.reshape(B, B), grad_neigh.reshape(B, B)


def solution(mesh):
    placed = (
        P("dom", None),
        P(None, "feat"),
        P(None, "feat"),
        P("dom", None, None),
        P("dom", None),
        P("dom"),
        P("dom", "feat"),
    )
    return jax.shard_map(
        on_device,
        mesh=mesh,
        in_specs=placed,
        out_specs=(P("dom", "feat"), P("dom", None), P(None, "feat"), P(None, "feat")),
        check_vma=False,
    )
```

time: 794 us -> 72.9 us (0.09)
  waiting for transfers between devices: 661 us -> 0 us
  Pallas kernels: 0 us -> 72.2 us
  matrix products: 35.7 us -> 0 us
  starting transfers between devices: 30.3 us -> 0 us
  local copies, waits for them, and re-layouts: 24.4 us -> 0 us
  other arithmetic: 15.9 us -> 0 us
  between operations: 14.2 us -> 0.64 us
    all_to_all x2 -> x0, waiting for transfers between devices: 363 us -> none  [the longest x1 363 us: on_device(): lax.all_to_all(partial_sums, 'dom', split_axis=0, concat_axis=0, tiled=True)]
    psum x1 -> x0, waiting for transfers between devices: 203 us -> none  [on_device(): weight_sum = lax.psum(local_term, 'dom')]
    all_gather x1 -> x0, waiting for transfers between devices: 95.2 us -> none  [on_device(): lax.all_gather(dagg, 'dom', axis=0, tiled=True)]
    pallas_call x0 -> x2, Pallas kernels: none -> 72.2 us  [the longest x1 65.1 us: on_device(): pl.pallas_call(kernel, out_shape=(jax.ShapeDtypeStruct((B, B), BF), jax.S...]
    dot_general x8 -> x0, matrix products: 35.7 us -> none  [the longest x1 9.29 us: on_device(): jnp.einsum('sij,ik->sjk', slot_tiles, message, preferred_element_type=jnp...]
    all_to_all x2 -> x0, starting transfers between devices: 30.2 us -> none  [the longest x1 16.3 us: on_device(): lax.all_to_all(slot_links, 'dom', split_axis=0, concat_axis=0, tiled=True)]
    reduce_sum x4 -> x0, other arithmetic: 14.3 us -> none  [the longest x1 6.85 us: on_device(): jnp.sum(slot_tiles.astype(jnp.float32), axis=1).reshape(peers, CAP * rows)]
    dot_general x1 -> x0, local copies, waits for them, and re-layouts: 11.9 us -> none  [on_device(): jnp.einsum('sij,ik->sjk', slot_tiles, message, preferred_element_type=jnp...]
  transfers between devices with their start and end apart: 4 -> 0, of which waited for: 3 -> 0; matrix products, arithmetic and copies ran while one was open for 4% -> 0% of each run, Pallas kernels for 0% -> 0%
where the time goes in v1:
time: 72.9 us; the launch traced here: 72.8 us
  Pallas kernels  72.2 us (99%)
    pallas_call x1, Pallas kernels, on_device(): pl.pallas_call(kernel, out_shape=(jax.ShapeDtypeStruct((B, B), BF), jax.S...  65.1 us
    pallas_call x1, Pallas kernels, on_device(): pl.pallas_call(hand_out, out_shape=tuple((jax.ShapeDtypeStruct(r.shape, r...  7.1 us

profile of v1, /device:TPU:1, one launch (start us, length us, event | category | flops | bytes accessed | tf_op | source)
XLA Modules:
  0.0 72.8 jit_solution(12123983026255768417)
XLA Ops:
  0.6 65.1 %sage.1 = (bf16[128,128]{1,0:T(8,128)(2,1)}, bf16[128,128]{1,0:T(8,128)(2,1)}, f32[2,4,16,128]{3,2,1,0:T(8,128)}, f32[2,4,16,128]{3,2,1,0:T(8,128)}) custom-call(bf16[128,128]{1,0:T(8,128)(2,1)} %feat_h.1, bf16[128,128]{1,0:T(8,128)(2,1)} %ws_h.1, bf16[128,128]{1,0:T(8,128)(2,1)} %wn_h.1, bf16[128,128,128]{2,1,0:T(8,128)(2,1)} %tiles_h.1, s32[1,128]{1,0:T(1,128)} %bitcast.4, ...), custom_call_target="tpu_custom_call" | custom-call | tf_op jit(solution)/shard_map/sage/pallas_call | solution.py:341
  65.7 7.1 %hand_out.1 = (bf16[128,128]{1,0:T(8,128)(2,1)}, bf16[128,128]{1,0:T(8,128)(2,1)}, f32[2,4,16,128]{3,2,1,0:T(8,128)}, f32[2,4,16,128]{3,2,1,0:T(8,128)}) custom-call(bf16[128,128]{1,0:T(8,128)(2,1)} %get-tuple-element.12.a, bf16[128,128]{1,0:T(8,128)(2,1)} %get-tuple-element.13.b, f32[2,4,16,128]{3,2,1,0:T(8,128)} %get-tuple-element.14.d, ...), custom_call_target="tpu_custom_call" | custom-call | tf_op jit(solution)/shard_map/hand_out/pallas_call | solution.py:406

commit v2 on v1

--- a/solution.py
+++ b/solution.py
@@ -57,6 +57,15 @@
 
     def take(ref, sem):
         pltpu.make_async_copy(ref, ref, sem).wait()
+
+    debts = []
+
+    def owe(ref, sem):
+        debts.append((ref, sem))
+
+    def settle():
+        for ref, sem in debts:
+            take(ref, sem)
 
     loads = [
         pltpu.make_async_copy(src, dst, load_sem.at[i])
@@ -128,6 +137,9 @@
         return carry
 
     lax.fori_loop(0, NZ, first_phase, 0)
+    owe(sx.at[:, pl.ds(0, 3)], s1.at[0])
+    owe(sy.at[:, pl.ds(0, 3)], s1.at[1])
+    owe(lk.at[pl.ds(0, 3)], sl.at[0])
     for k in SPREAD:
         push(lk.at[xp(k)], rlk1.at[k - 1], sl.at[0], rsl.at[0], dev(xp(k), y, z, c))
 
@@ -148,6 +160,9 @@
         return carry
 
     lax.fori_loop(0, NZ - 1, second_phase, 0)
+    owe(p1x.at[pl.ds(0, 7)], s2.at[0])
+    owe(p1y.at[pl.ds(0, 7)], s2.at[1])
+    owe(plk.at[pl.ds(0, 7)], sl.at[1])
     take(rlk1, rsl.at[0])
     plk[...] = lk[x] + rlk1[0] + rlk1[1] + rlk1[2]
     for p in range(NZ - 1):
@@ -183,6 +198,8 @@
         push(lk2, rlk3.at[k - 1], sl.at[2], rsl.at[2], dev(x, yp(k), z, c))
     r3[c * 4] = p2x[y]
     r3[8 + c * 4] = p2y[x]
+    owe(r3.at[pl.ds(0, 14)], s3)
+    owe(rlk3, sl.at[2])
     loads[6].wait()
     take(rlk3, rsl.at[2])
     links = lk2[pl.ds(y, 1), :]
@@ -212,53 +229,76 @@
     across = (((1,), (1,)), ((), ()))
     gpart[...] = lax.dot_general(wn[...], dpre, across, preferred_element_type=F32) * inverse
     push(gpart.at[pl.ds(pl.multiple_of(oc * 64, 64), 64)], grecv, sg.at[0], rsg.at[0], dev(x, y, z, oc))
+    owe(grecv, sg.at[0])
     grad_s = jnp.dot(xt[...], dpre, preferred_element_type=F32)
     grad_n = jnp.dot(mean_tb, dpre, preferred_element_type=F32)
     for k in range(2):
         w0[k] = grad_s[64 * k:64 * k + 64]
         w0[k + 2] = grad_n[64 * k:64 * k + 64]
+    for k in SPREAD:
+        push(w0.at[xp(k)], rw1.at[k - 1], sw.at[0], rw.at[0], dev(xp(k), y, z, c))
+    owe(rw1, sw.at[0])
     direct = lax.dot_general(dpre, ws[...], across, preferred_element_type=F32)
     take(grecv, rsg.at[0])
     gfull = (gpart[pl.ds(pl.multiple_of(c * 64, 64), 64), :] + grecv[...]).astype(BF)
     gx[0, x, y] = gfull[0:32]
     gy[0, y, x] = gfull[32:64]
 
-    for k in SPREAD:
-        push(gx.at[0, x, y], gx.at[0, x, y], sa.at[0], ra.at[0], dev(x, yp(k), z, c))
-        push(gy.at[0, y, x], gy.at[0, y, x], sa.at[1], ra.at[1], dev(xp(k), y, z, c))
-    for k in SPREAD:
-        push(w0.at[xp(k)], rw1.at[k - 1], sw.at[0], rw.at[0], dev(xp(k), y, z, c))
-
     near = (0, 7, 1, 6, 2, 5, 3, 4)
-    take(gx.at[0, x, pl.ds(0, 3)], ra.at[0])
     for q in range(1, NZ):
-        push(gx.at[0, x], gx.at[q, x], sb.at[0], rbx.at[q], dev(x, y, zp(NZ - near[q]), c))
-    take(gy.at[0, y, pl.ds(0, 3)], ra.at[1])
-    for q in range(1, NZ):
-        push(gy.at[0, y], gy.at[q, y], sb.at[1], rby.at[q], dev(x, y, zp(NZ - near[q]), c))
-
-    def forward(q):
+        to = dev(x, y, zp(NZ - near[q]), c)
+        push(gx.at[0, x, y], gx.at[q, x, y], sa.at[0], ra.at[q], to)
+        push(gy.at[0, y, x], gy.at[q, y, x], sa.at[1], ra.at[q], to)
+    owe(gx.at[0, 0, pl.ds(0, 4)], sa.at[0])
+    owe(gx.at[0, 0, pl.ds(0, 3)], sa.at[0])
+    owe(gy.at[0, 0, pl.ds(0, 4)], sa.at[1])
+    owe(gy.at[0, 0, pl.ds(0, 3)], sa.at[1])
+
+    def across_second(q):
         if q > 0:
-            take(gx.at[q, x], rbx.at[q])
+            take(gx.at[q, x, pl.ds(0, 2)], ra.at[q])
+        for k in SPREAD:
+            push(gx.at[q, x, y], gx.at[q, x, y], sb.at[0], rbx.at[q], dev(x, yp(k), z, c))
+            push(gy.at[q, y, x], gy.at[q, y, x], sb.at[1], rby.at[q], dev(xp(k), y, z, c))
+
+    def across_third(q):
+        take(gx.at[q, x, pl.ds(0, 3)], rbx.at[q])
         for k in SPREAD:
             push(gx.at[q, x], gx.at[q, x], sc.at[0], rcx.at[q], dev(xp(k), y, z, c))
-        if q > 0:
-            take(gy.at[q, y], rby.at[q])
+        take(gy.at[q, y, pl.ds(0, 3)], rby.at[q])
         for k in SPREAD:
             push(gy.at[q, y], gy.at[q, y], sc.at[1], rcy.at[q], dev(x, yp(k), z, c))
 
-    for q in range(0, 3):
-        forward(q)
+    across_second(0)
+    across_second(1)
+    across_second(2)
+    across_third(0)
     take(rw1, rw.at[0])
     w1[...] = (w0[x] + rw1[0] + rw1[1] + rw1[2]).reshape(4, 16, B)
     for k in SPREAD:
         push(w1.at[yp(k)], rw2.at[k - 1], sw.at[1], rw.at[1], dev(x, yp(k), z, c))
-    for q in range(3, NZ):
-        forward(q)
+    owe(rw2, sw.at[1])
+    across_second(3)
+    across_second(4)
+    across_third(1)
+    across_third(2)
+    across_second(5)
+    across_second(6)
     take(rw2, rw.at[1])
     rw3[z] = w1[y] + rw2[0] + rw2[1] + rw2[2]
     for k in range(1, NZ):
         push(rw3.at[z], rw3.at[z], sw.at[2], rw.at[2], dev(x, y, zp(k), c))
+    owe(rw3.at[pl.ds(0, 7)], sw.at[2])
+    across_third(3)
+    across_third(4)
+    across_second(7)
+    across_third(5)
+    across_third(6)
+    across_third(7)
+    owe(gx.at[:, 0, pl.ds(0, 3)], sb.at[0])
+    owe(gy.at[:, 0, pl.ds(0, 3)], sb.at[1])
+    owe(gx.at[:, pl.ds(0, 3)], sc.at[0])
+    owe(gy.at[:, pl.ds(0, 3)], sc.at[1])
 
     def last_phase(q, acc):
         take(gx.at[q, pl.ds(0, 3)], rcx.at[q])
@@ -270,7 +310,6 @@
             acc = acc + lax.dot_general(adj[NZ - 1 - q, py], right, across, preferred_element_type=F32)
         return acc
 
-    acc = lax.fori_loop(0, 3, last_phase, jnp.zeros((B, 64), F32))
     take(rw3.at[pl.ds(0, 7)], rw.at[2])
     total = rw3[0]
     for k in range(1, NZ):
@@ -278,12 +317,14 @@
     wg[x, y] = total
     for k in SPREAD:
         push(wg.at[x, y], wg.at[x, y], sw.at[3], rw.at[3], dev(x, yp(k), z, c))
-    acc = lax.fori_loop(3, 6, last_phase, acc)
+    acc = lax.fori_loop(0, 3, last_phase, jnp.zeros((B, 64), F32))
     take(wg.at[x, pl.ds(0, 3)], rw.at[3])
     for k in SPREAD:
         push(wg.at[x], wg.at[x], sw.at[4], rw.at[4], dev(xp(k), y, z, c))
-    acc = lax.fori_loop(6, 8, last_phase, acc)
-
+    acc = lax.fori_loop(3, 8, last_phase, acc)
+
+    owe(wg.at[0, pl.ds(0, 3)], sw.at[3])
+    owe(wg.at[pl.ds(0, 3)], sw.at[4])
     none = jnp.zeros((B, 64), F32)
     placed = jnp.where(c == 0, jnp.concatenate([acc, none], axis=1), jnp.concatenate([none, acc], axis=1))
     gis[...] = placed + direct
@@ -294,26 +335,7 @@
     emit[1].start()
     emit[2].start()
 
-    take(sx.at[:, pl.ds(0, 3)], s1.at[0])
-    take(sy.at[:, pl.ds(0, 3)], s1.at[1])
-    take(lk.at[pl.ds(0, 3)], sl.at[0])
-    take(p1x.at[pl.ds(0, 7)], s2.at[0])
-    take(p1y.at[pl.ds(0, 7)], s2.at[1])
-    take(plk.at[pl.ds(0, 7)], sl.at[1])
-    take(r3.at[pl.ds(0, 14)], s3)
-    take(rlk3, sl.at[2])
-    take(grecv, sg.at[0])
-    take(gx.at[0, 0, pl.ds(0, 3)], sa.at[0])
-    take(gy.at[0, 0, pl.ds(0, 3)], sa.at[1])
-    take(gx.at[pl.ds(0, 7), 0], sb.at[0])
-    take(gy.at[pl.ds(0, 7), 0], sb.at[1])
-    take(gx.at[:, pl.ds(0, 3)], sc.at[0])
-    take(gy.at[:, pl.ds(0, 3)], sc.at[1])
-    take(rw1, sw.at[0])
-    take(rw2, sw.at[1])
-    take(rw3.at[pl.ds(0, 7)], sw.at[2])
-    take(wg.at[0, pl.ds(0, 3)], sw.at[3])
-    take(wg.at[pl.ds(0, 3)], sw.at[4])
+    settle()
     take(gir, rsg.at[1])
     gi_o[...] = (gis[...] + gir[...]).astype(BF)
     emit.append(pltpu.make_async_copy(gi_o, gi_h, out_sem.at[3]))
@@ -323,14 +345,16 @@
         copy.wait()
 
 
-def hand_out(a, b, d, e, ao, bo, do, eo, sems):
-    copies = [
-        pltpu.make_async_copy(src, dst, sems.at[i])
-        for i, (src, dst) in enumerate(((a, ao), (b, bo), (d, do), (e, eo)))
-    ]
-    for copy in copies:
+def hand_out(*refs):
+    sources, targets, held, sems = refs[0:4], refs[4:8], refs[8:12], refs[12]
+    inward = [pltpu.make_async_copy(a, b, sems.at[0, i]) for i, (a, b) in enumerate(zip(sources, held))]
+    outward = [pltpu.make_async_copy(a, b, sems.at[1, i]) for i, (a, b) in enumerate(zip(held, targets))]
+    for copy in inward:
         copy.start()
-    for copy in copies:
+    for first, second in zip(inward, outward):
+        first.wait()
+        second.start()
+    for copy in outward:
         copy.wait()
 
 
@@ -392,7 +416,7 @@
             dma(()), dma(()),
             dma((3,)), dma((3,)),
             dma((2,)), dma((2,)),
-            dma((2,)), dma((2,)),
+            dma((2,)), dma((NZ,)),
             dma((2,)), dma((NZ,)), dma((NZ,)),
             dma((2,)), dma((NZ,)), dma((NZ,)),
             dma((5,)), dma((5,)),
@@ -408,7 +432,8 @@
         out_shape=tuple(jax.ShapeDtypeStruct(r.shape, r.dtype) for r in results),
         in_specs=[hbm] * 4,
         out_specs=(hbm,) * 4,
-        scratch_shapes=[dma((4,))],
+        scratch_shapes=[V(r.shape, r.dtype) for r in results] + [dma((2, 4))],
+        compiler_params=pltpu.CompilerParams(vmem_limit_bytes=60 * 2**20),
         name="hand_out",
     )(*results)
     output, grad_input, grad_self, grad_neigh = results

time: 72.9 us -> 62.2 us (0.85)
  Pallas kernels: 72.2 us -> 61.5 us
    pallas_call x1, Pallas kernels: 7.1 us -> 1.61 us  [on_device(): pl.pallas_call(hand_out, out_shape=tuple((jax.ShapeDtypeStruct(r.shape, r...]
    pallas_call x1, Pallas kernels: 65.1 us -> 59.8 us  [on_device(): pl.pallas_call(kernel, out_shape=(jax.ShapeDtypeStruct((B, B), BF), jax.S...]
where the time goes in v2:
time: 62.2 us; the launch traced here: 62.1 us
  Pallas kernels  61.5 us (99%)
  between operations  0.64 us (1%)
    pallas_call x1, Pallas kernels, on_device(): pl.pallas_call(kernel, out_shape=(jax.ShapeDtypeStruct((B, B), BF), jax.S...  59.8 us
    pallas_call x1, Pallas kernels, on_device(): pl.pallas_call(hand_out, out_shape=tuple((jax.ShapeDtypeStruct(r.shape, r...  1.61 us

profile of v2, /device:TPU:1, one launch (start us, length us, event | category | flops | bytes accessed | tf_op | source)
XLA Modules:
  0.0 62.1 jit_solution(11577361405119342227)
XLA Ops:
  0.6 59.8 %sage.1 = (bf16[128,128]{1,0:T(8,128)(2,1)}, bf16[128,128]{1,0:T(8,128)(2,1)}, f32[2,4,16,128]{3,2,1,0:T(8,128)}, f32[2,4,16,128]{3,2,1,0:T(8,128)}) custom-call(bf16[128,128]{1,0:T(8,128)(2,1)} %feat_h.1, bf16[128,128]{1,0:T(8,128)(2,1)} %ws_h.1, bf16[128,128]{1,0:T(8,128)(2,1)} %wn_h.1, bf16[128,128,128]{2,1,0:T(8,128)(2,1)} %tiles_h.1, s32[1,128]{1,0:T(1,128)} %bitcast.4, ...), custom_call_target="tpu_custom_call" | custom-call | tf_op jit(solution)/shard_map/sage/pallas_call | solution.py:365
  60.5 1.6 %hand_out.1 = (bf16[128,128]{1,0:T(8,128)(2,1)}, bf16[128,128]{1,0:T(8,128)(2,1)}, f32[2,4,16,128]{3,2,1,0:T(8,128)}, f32[2,4,16,128]{3,2,1,0:T(8,128)}) custom-call(bf16[128,128]{1,0:T(8,128)(2,1)} %get-tuple-element.12.refs_0_, bf16[128,128]{1,0:T(8,128)(2,1)} %get-tuple-element.13.refs_1_, f32[2,4,16,128]{3,2,1,0:T(8,128)} %get-tuple-element.14.refs_2_, ...), custom_call_target="tpu_custom_call" | custom-call | tf_op jit(solution)/shard_map/hand_out/pallas_call | solution.py:430

commit v3 on v2

--- a/solution.py
+++ b/solution.py
@@ -11,6 +11,8 @@
 NX, NY, NZ = 4, 4, 8
 B = 128
 SPREAD = (2, 1, 3)
+SLANTED = 0
+PLAN = ('s1', 's2', 't0', 'w2', 's3', 's4', 't1', 't2', 's5', 's6', 't3', 'w3', 's7', 'l0', 't4', 'l1', 't5', 'w4', 'l2', 't6', 'l3', 't7', 'w5', 'l4', 'l5', 'l6', 'l7')
 
 
 def far_first(p):
@@ -23,12 +25,12 @@
     out_h, gi_h, gs_h, gn_h,
     feat, ws, wn, dest, outside, cot, out_o, gi_o,
     tiles, adj, xt, idx_v, idx_s, selfp,
-    sx, sy, r1x, r1y, p1x, p1y, r2x, r2y, p2x, p2y, r3,
+    sx, sy, r1x, r1y, p1x, p1y, r2x, r2y, rpx, rpy, p2x, p2y, r3,
     lk, rlk1, plk, rlk2, lk2, rlk3,
     gpart, grecv, gx, gy,
     w0, rw1, w1, rw2, rw3, wg, gis, gir,
-    load_sem, s1, rs1x, rs1y, s2, rs2, s3, rs3, sl, rsl, sg, rsg,
-    sa, ra, sb, rbx, rby, sc, rcx, rcy, sw, rw, out_sem,
+    load_sem, s1, rs1x, rs1y, s2, rs2, rsp, s3, rs3, sl, rsl, sg, rsg,
+    sa, ra, sb, rbx, rby, sc, rcx, rcy, sw, rw, out_sem, past,
 ):
     dom = lax.axis_index("dom")
     c = lax.axis_index("feat")
@@ -71,26 +73,22 @@
         pltpu.make_async_copy(src, dst, load_sem.at[i])
         for i, (src, dst) in enumerate(
             (
-                (dest_h, dest), (tiles_h, tiles.at[pl.ds(0, B)]), (feat_h, feat), (ws_h, ws),
+                (dest_h, dest), (feat_h, feat), (ws_h, ws),
                 (wn_h, wn), (cot_h, cot), (outside_h, outside),
             )
         )
     ]
+    for i in range(4):
+        part = pl.ds(i * 32, 32)
+        loads.append(pltpu.make_async_copy(tiles_h.at[part], tiles.at[part], load_sem.at[7 + i]))
     for load in loads:
         load.start()
 
     barrier = pltpu.get_barrier_semaphore()
-    greeted = 0
-    for pc in (c, oc):
-        for k in (1, 2, 3):
-            for d in (dev(xp(k), y, z, pc), dev(x, yp(k), z, pc)):
-                pl.semaphore_signal(barrier, inc=1, device_id=d, device_id_type=MESH)
-                greeted += 1
-    for k in range(1, NZ):
-        pl.semaphore_signal(barrier, inc=1, device_id=dev(x, y, zp(k), c), device_id_type=MESH)
-        greeted += 1
-    pl.semaphore_signal(barrier, inc=1, device_id=dev(x, y, z, oc), device_id_type=MESH)
-    greeted += 1
+    line = [dev(xp(k), y, z, c) for k in (1, 2, 3)] + [dev(x, yp(k), z, c) for k in (1, 2, 3)]
+    line += [dev(x, y, zp(k), c) for k in range(1, NZ)] + [dev(x, y, z, oc)]
+    for d in line:
+        pl.semaphore_signal(barrier, inc=1, device_id=d, device_id_type=MESH)
 
     loads[0].wait()
     named = jnp.broadcast_to(dest[...], (B, B)).T
@@ -101,22 +99,23 @@
     first = jnp.min(jnp.where(hit, rows, B), axis=0, keepdims=True)
     idx_v[0:1, :] = first
     idx_v[1:2, :] = jnp.where(last > first, last, B)
-    table = pltpu.make_async_copy(idx_v, idx_s, load_sem.at[7])
+    table = pltpu.make_async_copy(idx_v, idx_s, load_sem.at[6])
     table.start()
     tiles[B] = jnp.zeros((B, B), BF)
-    loads[2].wait()
+    loads[1].wait()
     features = feat[...]
     xt[0:B, :] = features.astype(F32).T.astype(BF)
     xh = xt[pl.ds(pl.multiple_of(c * 64, 64), 64), :]
     left = jnp.concatenate([xh, jnp.ones((16, B), BF)], axis=0)
-    loads[3].wait()
+    loads[2].wait()
     selfp[...] = jnp.dot(features, ws[...], preferred_element_type=F32)
-    lk[...] = jnp.zeros_like(lk)
     table.wait()
-    loads[1].wait()
-    pl.semaphore_wait(barrier, greeted)
-
-    def first_phase(p, carry):
+    for load in loads[6:]:
+        load.wait()
+    pl.semaphore_wait(barrier, len(line))
+    pl.semaphore_signal(past, inc=1, device_id=dev(x, y, z, oc), device_id_type=MESH)
+
+    def first_phase(p):
         dz = zp(far_first(p))
         for py in range(NY):
             parts = []
@@ -130,18 +129,10 @@
                 part = o[:, px * B:(px + 1) * B]
                 sx[p, px, py] = part[0:32].astype(BF)
                 sy[p, py, px] = part[32:64].astype(BF)
-                lk[px, p, py:py + 1, :] = part[64:65]
+                lk[px + c * (py - px), p, pl.ds(py + c * (px - py), 1), :] = part[64:65]
         for k in SPREAD:
             push(sx.at[p, xp(k)], r1x.at[p, k - 1], s1.at[0], rs1x.at[p], dev(xp(k), y, z, c))
             push(sy.at[p, yp(k)], r1y.at[p, k - 1], s1.at[1], rs1y.at[p], dev(x, yp(k), z, c))
-        return carry
-
-    lax.fori_loop(0, NZ, first_phase, 0)
-    owe(sx.at[:, pl.ds(0, 3)], s1.at[0])
-    owe(sy.at[:, pl.ds(0, 3)], s1.at[1])
-    owe(lk.at[pl.ds(0, 3)], sl.at[0])
-    for k in SPREAD:
-        push(lk.at[xp(k)], rlk1.at[k - 1], sl.at[0], rsl.at[0], dev(xp(k), y, z, c))
 
     def add_four(own, got):
         total = own.astype(F32)
@@ -149,22 +140,45 @@
             total = total + got[k].astype(F32)
         return total
 
-    def second_phase(p, carry):
-        to = dev(x, y, zp(far_first(p)), c)
-        take(r1x.at[p], rs1x.at[p])
-        p1x[p] = add_four(sx[p, x], r1x.at[p]).astype(BF)
-        push(p1x.at[p], r2x.at[p], s2.at[0], rs2.at[0], to)
-        take(r1y.at[p], rs1y.at[p])
-        p1y[p] = add_four(sy[p, y], r1y.at[p]).astype(BF)
-        push(p1y.at[p], r2y.at[p], s2.at[1], rs2.at[1], to)
+    joins = {3: 0, 4: 1}
+    passed = {1: (1, 0), 2: (NZ - 1, 1)}
+    slots = {0: 0, 3: 1, 4: 2, 5: 3, 6: 4}
+
+    def second_phase(p):
+        for share, own, got, sent, s_, r_, ready, passed_on, r_passed in (
+            (0, sx.at[p, x], r1x, p1x, s2.at[0], r2x, rs1x, rpx, rsp),
+            (1, sy.at[p, y], r1y, p1y, s2.at[1], r2y, rs1y, rpy, rsp),
+        ):
+            take(got.at[p], ready.at[p])
+            total = add_four(own[...], got.at[p])
+            if p in joins:
+                take(passed_on.at[joins[p]], r_passed.at[share, joins[p]])
+                total = total + passed_on[joins[p]].astype(F32)
+            sent[p] = total.astype(BF)
+            if p in passed:
+                k, side = passed[p]
+                push(sent.at[p], passed_on.at[side], s_, r_passed.at[share, side], dev(x, y, zp(k), c))
+            else:
+                push(sent.at[p], r_.at[slots[p]], s_, rs2.at[share], dev(x, y, zp(far_first(p)), c))
+
+    def each_first(p, carry):
+        first_phase(p)
         return carry
 
-    lax.fori_loop(0, NZ - 1, second_phase, 0)
+    lax.fori_loop(0, NZ, each_first, 0)
+    for k in SPREAD:
+        to = dev(x + oc * (xp(k) - x), y + c * (yp(k) - y), z, c)
+        push(lk.at[xp(k) + c * (yp(k) - xp(k))], rlk1.at[k - 1], sl.at[0], rsl.at[0], to)
+    for p in range(NZ - 1):
+        second_phase(p)
+    owe(sx.at[:, pl.ds(0, 3)], s1.at[0])
+    owe(sy.at[:, pl.ds(0, 3)], s1.at[1])
+    owe(lk.at[pl.ds(0, 3)], sl.at[0])
     owe(p1x.at[pl.ds(0, 7)], s2.at[0])
     owe(p1y.at[pl.ds(0, 7)], s2.at[1])
     owe(plk.at[pl.ds(0, 7)], sl.at[1])
     take(rlk1, rsl.at[0])
-    plk[...] = lk[x] + rlk1[0] + rlk1[1] + rlk1[2]
+    plk[...] = lk[x + c * (y - x)] + rlk1[0] + rlk1[1] + rlk1[2]
     for p in range(NZ - 1):
         push(plk.at[p], rlk2.at[p], sl.at[1], rsl.at[1], dev(x, y, zp(far_first(p)), c))
     own = NZ - 1
@@ -173,17 +187,18 @@
     take(r1y.at[own], rs1y.at[own])
     keep_y = add_four(sy[own, y], r1y.at[own])
 
+    pl.semaphore_wait(past, 1)
     take(r2x, rs2.at[0])
-    for p in range(NZ - 1):
-        keep_x = keep_x + r2x[p].astype(F32)
+    for i in range(5):
+        keep_x = keep_x + r2x[i].astype(F32)
     p2x[...] = keep_x.astype(BF)
     for pc in (c, oc):
         for k in SPREAD:
             push(p2x.at[yp(k)], r3.at[c * 4 + k], s3, rs3, dev(x, yp(k), z, pc))
     push(p2x.at[y], r3.at[c * 4], s3, rs3, dev(x, y, z, oc))
     take(r2y, rs2.at[1])
-    for p in range(NZ - 1):
-        keep_y = keep_y + r2y[p].astype(F32)
+    for i in range(5):
+        keep_y = keep_y + r2y[i].astype(F32)
     p2y[...] = keep_y.astype(BF)
     for pc in (c, oc):
         for k in SPREAD:
@@ -195,16 +210,18 @@
         total = total + rlk2[p]
     lk2[...] = total
     for k in SPREAD:
-        push(lk2, rlk3.at[k - 1], sl.at[2], rsl.at[2], dev(x, yp(k), z, c))
+        to = dev(x + c * (xp(k) - x), y + oc * (yp(k) - y), z, c)
+        push(lk2, rlk3.at[k - 1], sl.at[2], rsl.at[2], to)
     r3[c * 4] = p2x[y]
     r3[8 + c * 4] = p2y[x]
     owe(r3.at[pl.ds(0, 14)], s3)
     owe(rlk3, sl.at[2])
-    loads[6].wait()
+    loads[5].wait()
     take(rlk3, rsl.at[2])
-    links = lk2[pl.ds(y, 1), :]
+    row = pl.ds(y + c * (x - y), 1)
+    links = lk2[row, :]
     for k in range(3):
-        links = links + rlk3[k, pl.ds(y, 1), :]
+        links = links + rlk3[k, row, :]
     inverse = 1.0 / (links + outside[...].astype(F32))
     take(r3.at[pl.ds(0, 14)], rs3)
     pieces = []
@@ -218,8 +235,8 @@
     mean_t = jnp.concatenate(pieces, axis=0) * inverse
     mean_tb = mean_t.astype(BF)
 
+    loads[3].wait()
     loads[4].wait()
-    loads[5].wait()
     pre = selfp[...] + jnp.dot(mean_t.T.astype(BF), wn[...], preferred_element_type=F32)
     sigma = jax.nn.sigmoid(pre)
     out_o[...] = (pre * sigma).astype(BF)
@@ -232,11 +249,11 @@
     owe(grecv, sg.at[0])
     grad_s = jnp.dot(xt[...], dpre, preferred_element_type=F32)
     grad_n = jnp.dot(mean_tb, dpre, preferred_element_type=F32)
-    for k in range(2):
-        w0[k] = grad_s[64 * k:64 * k + 64]
-        w0[k + 2] = grad_n[64 * k:64 * k + 64]
+    w0[0] = grad_s.reshape(4, 32, B)
+    w0[1] = grad_n.reshape(4, 32, B)
     for k in SPREAD:
-        push(w0.at[xp(k)], rw1.at[k - 1], sw.at[0], rw.at[0], dev(xp(k), y, z, c))
+        push(w0.at[0, xp(k)], rw1.at[k - 1], sw.at[0], rw.at[0], dev(xp(k), y, z, c))
+        push(w0.at[1, yp(k)], rw1.at[k + 2], sw.at[0], rw.at[0], dev(x, yp(k), z, c))
     owe(rw1, sw.at[0])
     direct = lax.dot_general(dpre, ws[...], across, preferred_element_type=F32)
     take(grecv, rsg.at[0])
@@ -245,60 +262,39 @@
     gy[0, y, x] = gfull[32:64]
 
     near = (0, 7, 1, 6, 2, 5, 3, 4)
+    def along_second(q):
+        there = zp(NZ - near[q])
+        for k in SPREAD:
+            push(gx.at[0, x, y], gx.at[q, x, y], sb.at[0], rbx.at[q], dev(x, yp(k), there, c))
+            push(gy.at[0, y, x], gy.at[q, y, x], sb.at[1], rby.at[q], dev(xp(k), y, there, c))
+
+    along_second(0)
     for q in range(1, NZ):
         to = dev(x, y, zp(NZ - near[q]), c)
         push(gx.at[0, x, y], gx.at[q, x, y], sa.at[0], ra.at[q], to)
         push(gy.at[0, y, x], gy.at[q, y, x], sa.at[1], ra.at[q], to)
+        if q <= SLANTED:
+            along_second(q)
     owe(gx.at[0, 0, pl.ds(0, 4)], sa.at[0])
     owe(gx.at[0, 0, pl.ds(0, 3)], sa.at[0])
     owe(gy.at[0, 0, pl.ds(0, 4)], sa.at[1])
     owe(gy.at[0, 0, pl.ds(0, 3)], sa.at[1])
 
     def across_second(q):
-        if q > 0:
-            take(gx.at[q, x, pl.ds(0, 2)], ra.at[q])
+        take(gx.at[q, x, pl.ds(0, 2)], ra.at[q])
         for k in SPREAD:
             push(gx.at[q, x, y], gx.at[q, x, y], sb.at[0], rbx.at[q], dev(x, yp(k), z, c))
             push(gy.at[q, y, x], gy.at[q, y, x], sb.at[1], rby.at[q], dev(xp(k), y, z, c))
 
     def across_third(q):
+        if 0 < q <= SLANTED:
+            take(gx.at[q, x, pl.ds(0, 2)], ra.at[q])
         take(gx.at[q, x, pl.ds(0, 3)], rbx.at[q])
         for k in SPREAD:
             push(gx.at[q, x], gx.at[q, x], sc.at[0], rcx.at[q], dev(xp(k), y, z, c))
         take(gy.at[q, y, pl.ds(0, 3)], rby.at[q])
         for k in SPREAD:
             push(gy.at[q, y], gy.at[q, y], sc.at[1], rcy.at[q], dev(x, yp(k), z, c))
-
-    across_second(0)
-    across_second(1)
-    across_second(2)
-    across_third(0)
-    take(rw1, rw.at[0])
-    w1[...] = (w0[x] + rw1[0] + rw1[1] + rw1[2]).reshape(4, 16, B)
-    for k in SPREAD:
-        push(w1.at[yp(k)], rw2.at[k - 1], sw.at[1], rw.at[1], dev(x, yp(k), z, c))
-    owe(rw2, sw.at[1])
-    across_second(3)
-    across_second(4)
-    across_third(1)
-    across_third(2)
-    across_second(5)
-    across_second(6)
-    take(rw2, rw.at[1])
-    rw3[z] = w1[y] + rw2[0] + rw2[1] + rw2[2]
-    for k in range(1, NZ):
-        push(rw3.at[z], rw3.at[z], sw.at[2], rw.at[2], dev(x, y, zp(k), c))
-    owe(rw3.at[pl.ds(0, 7)], sw.at[2])
-    across_third(3)
-    across_third(4)
-    across_second(7)
-    across_third(5)
-    across_third(6)
-    across_third(7)
-    owe(gx.at[:, 0, pl.ds(0, 3)], sb.at[0])
-    owe(gy.at[:, 0, pl.ds(0, 3)], sb.at[1])
-    owe(gx.at[:, pl.ds(0, 3)], sc.at[0])
-    owe(gy.at[:, pl.ds(0, 3)], sc.at[1])
 
     def last_phase(q, acc):
         take(gx.at[q, pl.ds(0, 3)], rcx.at[q])
@@ -310,28 +306,69 @@
             acc = acc + lax.dot_general(adj[NZ - 1 - q, py], right, across, preferred_element_type=F32)
         return acc
 
-    take(rw3.at[pl.ds(0, 7)], rw.at[2])
-    total = rw3[0]
-    for k in range(1, NZ):
-        total = total + rw3[k]
-    wg[x, y] = total
-    for k in SPREAD:
-        push(wg.at[x, y], wg.at[x, y], sw.at[3], rw.at[3], dev(x, yp(k), z, c))
-    acc = lax.fori_loop(0, 3, last_phase, jnp.zeros((B, 64), F32))
-    take(wg.at[x, pl.ds(0, 3)], rw.at[3])
-    for k in SPREAD:
-        push(wg.at[x], wg.at[x], sw.at[4], rw.at[4], dev(xp(k), y, z, c))
-    acc = lax.fori_loop(3, 8, last_phase, acc)
-
-    owe(wg.at[0, pl.ds(0, 3)], sw.at[3])
-    owe(wg.at[pl.ds(0, 3)], sw.at[4])
+    def weights_second():
+        take(rw1, rw.at[0])
+        for share, own in ((0, x), (1, y)):
+            part = w0[share, own]
+            for k in range(3):
+                part = part + rw1[3 * share + k]
+            w1[share] = part.reshape(4, 8, B)
+        for k in SPREAD:
+            push(w1.at[0, yp(k)], rw2.at[k - 1], sw.at[1], rw.at[1], dev(x, yp(k), z, c))
+            push(w1.at[1, xp(k)], rw2.at[k + 2], sw.at[1], rw.at[1], dev(xp(k), y, z, c))
+        owe(rw2, sw.at[1])
+
+    def weights_third():
+        take(rw2, rw.at[1])
+        rw3[z, 0] = w1[0, y] + rw2[0] + rw2[1] + rw2[2]
+        rw3[z, 1] = w1[1, x] + rw2[3] + rw2[4] + rw2[5]
+        for k in range(1, NZ):
+            push(rw3.at[z], rw3.at[z], sw.at[2], rw.at[2], dev(x, y, zp(k), c))
+        owe(rw3.at[pl.ds(0, 7)], sw.at[2])
+
+    def weights_fourth():
+        take(rw3.at[pl.ds(0, 7)], rw.at[2])
+        total = rw3[0]
+        for k in range(1, NZ):
+            total = total + rw3[k]
+        wg[0, x, y] = total[0]
+        wg[1, y, x] = total[1]
+        for k in SPREAD:
+            push(wg.at[0, x, y], wg.at[0, x, y], sw.at[3], rw.at[3], dev(x, yp(k), z, c))
+            push(wg.at[1, y, x], wg.at[1, y, x], sw.at[3], rw.at[3], dev(xp(k), y, z, c))
+        owe(rw2, sw.at[3])
+
+    def weights_fifth():
+        take(rw2, rw.at[3])
+        for k in SPREAD:
+            push(wg.at[0, x], wg.at[0, x], sw.at[4], rw.at[4], dev(xp(k), y, z, c))
+            push(wg.at[1, y], wg.at[1, y], sw.at[4], rw.at[4], dev(x, yp(k), z, c))
+        owe(rw1, sw.at[4])
+
+    acc = jnp.zeros((B, 64), F32)
+    weights = {2: weights_second, 3: weights_third, 4: weights_fourth, 5: weights_fifth}
+    for step in PLAN:
+        what, q = step[0], int(step[1])
+        if what == "s":
+            across_second(q)
+        elif what == "t":
+            across_third(q)
+        elif what == "w":
+            weights[q]()
+        else:
+            acc = last_phase(q, acc)
+    owe(gx.at[:, 0, pl.ds(0, 3)], sb.at[0])
+    owe(gy.at[:, 0, pl.ds(0, 3)], sb.at[1])
+    owe(gx.at[:, pl.ds(0, 3)], sc.at[0])
+    owe(gy.at[:, pl.ds(0, 3)], sc.at[1])
+
     none = jnp.zeros((B, 64), F32)
     placed = jnp.where(c == 0, jnp.concatenate([acc, none], axis=1), jnp.concatenate([none, acc], axis=1))
     gis[...] = placed + direct
     push(gis, gir, sg.at[1], rsg.at[1], dev(x, y, z, oc))
-    take(wg.at[pl.ds(0, 3)], rw.at[4])
-    emit.append(pltpu.make_async_copy(wg.at[pl.ds(0, 2)], gs_h, out_sem.at[1]))
-    emit.append(pltpu.make_async_copy(wg.at[pl.ds(2, 2)], gn_h, out_sem.at[2]))
+    take(rw1, rw.at[4])
+    emit.append(pltpu.make_async_copy(wg.at[0], gs_h, out_sem.at[1]))
+    emit.append(pltpu.make_async_copy(wg.at[1], gn_h, out_sem.at[2]))
     emit[1].start()
     emit[2].start()
 
@@ -367,8 +404,8 @@
         out_shape=(
             jax.ShapeDtypeStruct((B, B), BF),
             jax.ShapeDtypeStruct((B, B), BF),
-            jax.ShapeDtypeStruct((2, NY, 16, B), F32),
-            jax.ShapeDtypeStruct((2, NY, 16, B), F32),
+            jax.ShapeDtypeStruct((4, 4, 8, B), F32),
+            jax.ShapeDtypeStruct((4, 4, 8, B), F32),
         ),
         in_specs=[hbm] * 7,
         out_specs=(hbm,) * 4,
@@ -387,32 +424,34 @@
             V((NZ, 3, NX, 32, B), BF),
             V((NZ, NY, 32, B), BF),
             V((NZ, NX, 32, B), BF),
-            V((NZ - 1, NY, 32, B), BF),
-            V((NZ - 1, NX, 32, B), BF),
+            V((5, NY, 32, B), BF),
+            V((5, NX, 32, B), BF),
+            V((2, NY, 32, B), BF),
+            V((2, NX, 32, B), BF),
             V((NY, 32, B), BF),
             V((NX, 32, B), BF),
             V((16, 32, B), BF),
-            V((NX, NZ, 8, B), F32),
-            V((3, NZ, 8, B), F32),
-            V((NZ, 8, B), F32),
-            V((NZ - 1, 8, B), F32),
-            V((8, B), F32),
-            V((3, 8, B), F32),
+            V((NX, NZ, 4, B), F32),
+            V((3, NZ, 4, B), F32),
+            V((NZ, 4, B), F32),
+            V((NZ - 1, 4, B), F32),
+            V((4, B), F32),
+            V((3, 4, B), F32),
             V((B, B), F32),
             V((64, B), F32),
             V((NZ, NX, NY, 32, B), BF),
             V((NZ, NY, NX, 32, B), BF),
-            V((4, 64, B), F32),
-            V((3, 64, B), F32),
-            V((4, 16, B), F32),
-            V((3, 16, B), F32),
-            V((NZ, 16, B), F32),
-            V((NX, NY, 16, B), F32),
+            V((2, 4, 32, B), F32),
+            V((6, 32, B), F32),
+            V((2, 4, 8, B), F32),
+            V((6, 8, B), F32),
+            V((NZ, 2, 8, B), F32),
+            V((2, 4, 4, 8, B), F32),
             V((B, B), F32),
             V((B, B), F32),
-            dma((8,)),
+            dma((11,)),
             dma((2,)), dma((NZ,)), dma((NZ,)),
-            dma((2,)), dma((2,)),
+            dma((2,)), dma((2,)), dma((2, 2)),
             dma(()), dma(()),
             dma((3,)), dma((3,)),
             dma((2,)), dma((2,)),
@@ -421,6 +460,7 @@
             dma((2,)), dma((NZ,)), dma((NZ,)),
             dma((5,)), dma((5,)),
             dma((4,)),
+            pltpu.SemaphoreType.REGULAR,
         ],
         compiler_params=pltpu.CompilerParams(
             collective_id=0, has_side_effects=True, vmem_limit_bytes=60 * 2**20

time: 62.2 us -> 61 us (0.981)
  Pallas kernels: 61.5 us -> 60.2 us
    pallas_call x1, Pallas kernels: 59.8 us -> 58.6 us  [on_device(): pl.pallas_call(kernel, out_shape=(jax.ShapeDtypeStruct((B, B), BF), jax.S...]
where the time goes in v3:
time: 61 us; the launch traced here: 60.8 us
  Pallas kernels  60.2 us (99%)
  between operations  0.64 us (1%)
    pallas_call x1, Pallas kernels, on_device(): pl.pallas_call(kernel, out_shape=(jax.ShapeDtypeStruct((B, B), BF), jax.S...  58.6 us
    pallas_call x1, Pallas kernels, on_device(): pl.pallas_call(hand_out, out_shape=tuple((jax.ShapeDtypeStruct(r.shape, r...  1.61 us

profile of v3, /device:TPU:1, one launch (start us, length us, event | category | flops | bytes accessed | tf_op | source)
XLA Modules:
  0.0 60.8 jit_solution(6218558050403608266)
XLA Ops:
  0.6 58.6 %sage.1 = (bf16[128,128]{1,0:T(8,128)(2,1)}, bf16[128,128]{1,0:T(8,128)(2,1)}, f32[4,4,8,128]{3,2,1,0:T(8,128)}, f32[4,4,8,128]{3,2,1,0:T(8,128)}) custom-call(bf16[128,128]{1,0:T(8,128)(2,1)} %feat_h.1, bf16[128,128]{1,0:T(8,128)(2,1)} %ws_h.1, bf16[128,128]{1,0:T(8,128)(2,1)} %wn_h.1, bf16[128,128,128]{2,1,0:T(8,128)(2,1)} %tiles_h.1, s32[1,128]{1,0:T(1,128)} %bitcast.4, ...), custom_call_target="tpu_custom_call" | custom-call | tf_op jit(solution)/shard_map/sage/pallas_call | solution.py:402
  59.2 1.6 %hand_out.1 = (bf16[128,128]{1,0:T(8,128)(2,1)}, bf16[128,128]{1,0:T(8,128)(2,1)}, f32[4,4,8,128]{3,2,1,0:T(8,128)}, f32[4,4,8,128]{3,2,1,0:T(8,128)}) custom-call(bf16[128,128]{1,0:T(8,128)(2,1)} %get-tuple-element.12.refs_0_, bf16[128,128]{1,0:T(8,128)(2,1)} %get-tuple-element.13.refs_1_, f32[4,4,8,128]{3,2,1,0:T(8,128)} %get-tuple-element.14.refs_2_, ...), custom_call_target="tpu_custom_call" | custom-call | tf_op jit(solution)/shard_map/hand_out/pallas_call | solution.py:470

commit v4 on v3

--- a/solution.py
+++ b/solution.py
@@ -11,13 +11,12 @@
 NX, NY, NZ = 4, 4, 8
 B = 128
 SPREAD = (2, 1, 3)
-SLANTED = 0
-PLAN = ('s1', 's2', 't0', 'w2', 's3', 's4', 't1', 't2', 's5', 's6', 't3', 'w3', 's7', 'l0', 't4', 'l1', 't5', 'w4', 'l2', 't6', 'l3', 't7', 'w5', 'l4', 'l5', 'l6', 'l7')
-
-
-def far_first(p):
-    half = (p + 1) // 2
-    return 4 + half * (1 - 2 * (p % 2))
+PLAN = ('s3', 's4', 't0', 's5', 's6', 'w2', 's7', 't3', 't4', 'r0', 't5', 't6', 'l0', 'w3', 't7', 'l3', 'l4', 'l5', 'l6', 'l1', 'l2', 'l7')
+
+
+STEPS = (1, 7, 3, 5, 4, 2, 6, 0)
+OWN = 7
+PACKED = sum(step * 8**i for i, step in enumerate(STEPS))
 
 
 def kernel(
@@ -25,11 +24,11 @@
     out_h, gi_h, gs_h, gn_h,
     feat, ws, wn, dest, outside, cot, out_o, gi_o,
     tiles, adj, xt, idx_v, idx_s, selfp,
-    sx, sy, r1x, r1y, p1x, p1y, r2x, r2y, rpx, rpy, p2x, p2y, r3,
+    sx, sy, r1x, r1y, p1x, p1y, r2x, r2y, rawx, rawy, rawl, rpx, rpy, p2x, p2y, r3,
     lk, rlk1, plk, rlk2, lk2, rlk3,
     gpart, grecv, gx, gy,
-    w0, rw1, w1, rw2, rw3, wg, gis, gir,
-    load_sem, s1, rs1x, rs1y, s2, rs2, rsp, s3, rs3, sl, rsl, sg, rsg,
+    w0, rw1, rw3, wg, gis, gir,
+    load_sem, s1, rraw, rs1x, rs1y, s2, rs2, rsp, s3, rs3, sl, rsl, rsl1, sg, rsg,
     sa, ra, sb, rbx, rby, sc, rcx, rcy, sw, rw, out_sem, past,
 ):
     dom = lax.axis_index("dom")
@@ -115,12 +114,12 @@
     pl.semaphore_wait(barrier, len(line))
     pl.semaphore_signal(past, inc=1, device_id=dev(x, y, z, oc), device_id_type=MESH)
 
-    def first_phase(p):
-        dz = zp(far_first(p))
+    def partial_sums(p, dz):
+        to_z = zp(dz)
         for py in range(NY):
             parts = []
             for px in range(NX):
-                d = (py * NZ + dz) * NX + px
+                d = (py * NZ + to_z) * NX + px
                 both = tiles[idx_s[0, d]] + tiles[idx_s[1, d]]
                 adj[p, py, :, px * B:(px + 1) * B] = both
                 parts.append(both)
@@ -129,10 +128,43 @@
                 part = o[:, px * B:(px + 1) * B]
                 sx[p, px, py] = part[0:32].astype(BF)
                 sy[p, py, px] = part[32:64].astype(BF)
-                lk[px + c * (py - px), p, pl.ds(py + c * (px - py), 1), :] = part[64:65]
+                lk[p, px + c * (py - px), pl.ds(py + c * (px - py), 1), :] = part[64:65]
+
+    def send_first(p):
         for k in SPREAD:
             push(sx.at[p, xp(k)], r1x.at[p, k - 1], s1.at[0], rs1x.at[p], dev(xp(k), y, z, c))
             push(sy.at[p, yp(k)], r1y.at[p, k - 1], s1.at[1], rs1y.at[p], dev(x, yp(k), z, c))
+        for k in SPREAD:
+            to = dev(x + oc * (xp(k) - x), y + c * (yp(k) - y), z, c)
+            push(lk.at[p, xp(k) + c * (yp(k) - xp(k))], rlk1.at[p, k - 1], sl.at[0], rsl1.at[p], to)
+
+    def to_next(p, code):
+        dz = lax.rem(code, 8)
+        partial_sums(p, dz)
+        to = dev(x, y, zp(dz), c)
+        push(sx.at[p], rawx.at[p], s1.at[2], rraw.at[0], to)
+        push(sy.at[p], rawy.at[p], s1.at[3], rraw.at[1], to)
+        push(lk.at[p], rawl.at[p], s1.at[4], rraw.at[2], to)
+        return code // 8
+
+    def to_far(p, code):
+        partial_sums(p, lax.rem(code, 8))
+        send_first(p)
+        return code // 8
+
+    lax.fori_loop(0, 2, to_next, PACKED)
+    lax.fori_loop(2, OWN, to_far, PACKED // 64)
+    partial_sums(OWN, 0)
+
+    def send_own():
+        for sent, raw, i in ((sx, rawx, 0), (sy, rawy, 1)):
+            take(raw, rraw.at[i])
+            for k in range(4):
+                total = sent[OWN, k].astype(F32) + raw[0, k].astype(F32) + raw[1, k].astype(F32)
+                sent[OWN, k] = total.astype(BF)
+        take(rawl, rraw.at[2])
+        lk[OWN] = lk[OWN] + rawl[0] + rawl[1]
+        send_first(OWN)
 
     def add_four(own, got):
         total = own.astype(F32)
@@ -140,9 +172,13 @@
             total = total + got[k].astype(F32)
         return total
 
-    joins = {3: 0, 4: 1}
-    passed = {1: (1, 0), 2: (NZ - 1, 1)}
-    slots = {0: 0, 3: 1, 4: 2, 5: 3, 6: 4}
+    joins = {5: 0, 6: 1}
+    passed = {2: (1, 0), 3: (NZ - 1, 1)}
+    slots = {4: 0, 5: 1, 6: 2}
+
+    def sum_links(p):
+        take(rlk1.at[p], rsl1.at[p])
+        plk[p] = lk[p, x + c * (y - x)] + rlk1[p, 0] + rlk1[p, 1] + rlk1[p, 2]
 
     def second_phase(p):
         for share, own, got, sent, s_, r_, ready, passed_on, r_passed in (
@@ -159,29 +195,25 @@
                 k, side = passed[p]
                 push(sent.at[p], passed_on.at[side], s_, r_passed.at[share, side], dev(x, y, zp(k), c))
             else:
-                push(sent.at[p], r_.at[slots[p]], s_, rs2.at[share], dev(x, y, zp(far_first(p)), c))
-
-    def each_first(p, carry):
-        first_phase(p)
-        return carry
-
-    lax.fori_loop(0, NZ, each_first, 0)
-    for k in SPREAD:
-        to = dev(x + oc * (xp(k) - x), y + c * (yp(k) - y), z, c)
-        push(lk.at[xp(k) + c * (yp(k) - xp(k))], rlk1.at[k - 1], sl.at[0], rsl.at[0], to)
-    for p in range(NZ - 1):
+                push(sent.at[p], r_.at[slots[p]], s_, rs2.at[share], dev(x, y, zp(STEPS[p]), c))
+
+    for p in range(2, OWN):
         second_phase(p)
-    owe(sx.at[:, pl.ds(0, 3)], s1.at[0])
-    owe(sy.at[:, pl.ds(0, 3)], s1.at[1])
-    owe(lk.at[pl.ds(0, 3)], sl.at[0])
-    owe(p1x.at[pl.ds(0, 7)], s2.at[0])
-    owe(p1y.at[pl.ds(0, 7)], s2.at[1])
-    owe(plk.at[pl.ds(0, 7)], sl.at[1])
-    take(rlk1, rsl.at[0])
-    plk[...] = lk[x + c * (y - x)] + rlk1[0] + rlk1[1] + rlk1[2]
-    for p in range(NZ - 1):
-        push(plk.at[p], rlk2.at[p], sl.at[1], rsl.at[1], dev(x, y, zp(far_first(p)), c))
-    own = NZ - 1
+        sum_links(p)
+        push(plk.at[p], rlk2.at[p - 2], sl.at[1], rsl.at[1], dev(x, y, zp(STEPS[p]), c))
+        if p == 3:
+            send_own()
+    owe(sx.at[pl.ds(2, 6), pl.ds(0, 3)], s1.at[0])
+    owe(sy.at[pl.ds(2, 6), pl.ds(0, 3)], s1.at[1])
+    owe(rawx, s1.at[2])
+    owe(rawy, s1.at[3])
+    owe(rawl, s1.at[4])
+    owe(lk.at[pl.ds(2, 6), pl.ds(0, 3)], sl.at[0])
+    owe(p1x.at[pl.ds(0, 5)], s2.at[0])
+    owe(p1y.at[pl.ds(0, 5)], s2.at[1])
+    owe(plk.at[pl.ds(0, 5)], sl.at[1])
+    own = OWN
+    sum_links(own)
     take(r1x.at[own], rs1x.at[own])
     keep_x = add_four(sx[own, x], r1x.at[own])
     take(r1y.at[own], rs1y.at[own])
@@ -189,7 +221,7 @@
 
     pl.semaphore_wait(past, 1)
     take(r2x, rs2.at[0])
-    for i in range(5):
+    for i in range(3):
         keep_x = keep_x + r2x[i].astype(F32)
     p2x[...] = keep_x.astype(BF)
     for pc in (c, oc):
@@ -197,7 +229,7 @@
             push(p2x.at[yp(k)], r3.at[c * 4 + k], s3, rs3, dev(x, yp(k), z, pc))
     push(p2x.at[y], r3.at[c * 4], s3, rs3, dev(x, y, z, oc))
     take(r2y, rs2.at[1])
-    for i in range(5):
+    for i in range(3):
         keep_y = keep_y + r2y[i].astype(F32)
     p2y[...] = keep_y.astype(BF)
     for pc in (c, oc):
@@ -206,8 +238,8 @@
     push(p2y.at[x], r3.at[8 + c * 4], s3, rs3, dev(x, y, z, oc))
     take(rlk2, rsl.at[1])
     total = plk[own]
-    for p in range(NZ - 1):
-        total = total + rlk2[p]
+    for i in range(5):
+        total = total + rlk2[i]
     lk2[...] = total
     for k in SPREAD:
         to = dev(x + c * (xp(k) - x), y + oc * (yp(k) - y), z, c)
@@ -249,12 +281,13 @@
     owe(grecv, sg.at[0])
     grad_s = jnp.dot(xt[...], dpre, preferred_element_type=F32)
     grad_n = jnp.dot(mean_tb, dpre, preferred_element_type=F32)
-    w0[0] = grad_s.reshape(4, 32, B)
-    w0[1] = grad_n.reshape(4, 32, B)
-    for k in SPREAD:
-        push(w0.at[0, xp(k)], rw1.at[k - 1], sw.at[0], rw.at[0], dev(xp(k), y, z, c))
-        push(w0.at[1, yp(k)], rw1.at[k + 2], sw.at[0], rw.at[0], dev(x, yp(k), z, c))
-    owe(rw1, sw.at[0])
+    w0[:, 0:8, :] = grad_s.reshape(16, 8, B)
+    w0[:, 8:16, :] = grad_n.reshape(16, 8, B)
+    here = x * NY + y
+    plane = [(i, j) for i in (2, 1, 3, 0) for j in (2, 1, 3, 0) if (i, j) != (0, 0)]
+    for i, j in plane:
+        push(w0.at[xp(i) * NY + yp(j)], rw1.at[here], sw.at[0], rw.at[0], dev(xp(i), yp(j), z, c))
+    owe(rw1.at[pl.ds(0, 15)], sw.at[0])
     direct = lax.dot_general(dpre, ws[...], across, preferred_element_type=F32)
     take(grecv, rsg.at[0])
     gfull = (gpart[pl.ds(pl.multiple_of(c * 64, 64), 64), :] + grecv[...]).astype(BF)
@@ -262,23 +295,15 @@
     gy[0, y, x] = gfull[32:64]
 
     near = (0, 7, 1, 6, 2, 5, 3, 4)
-    def along_second(q):
-        there = zp(NZ - near[q])
-        for k in SPREAD:
-            push(gx.at[0, x, y], gx.at[q, x, y], sb.at[0], rbx.at[q], dev(x, yp(k), there, c))
-            push(gy.at[0, y, x], gy.at[q, y, x], sb.at[1], rby.at[q], dev(xp(k), y, there, c))
-
-    along_second(0)
-    for q in range(1, NZ):
+    for k in SPREAD:
+        push(gx.at[0, x, y], gx.at[0, x, y], sb.at[0], rbx.at[0], dev(x, yp(k), z, c))
+        push(gy.at[0, y, x], gy.at[0, y, x], sb.at[1], rby.at[0], dev(xp(k), y, z, c))
+    for q in range(3, NZ):
         to = dev(x, y, zp(NZ - near[q]), c)
         push(gx.at[0, x, y], gx.at[q, x, y], sa.at[0], ra.at[q], to)
         push(gy.at[0, y, x], gy.at[q, y, x], sa.at[1], ra.at[q], to)
-        if q <= SLANTED:
-            along_second(q)
-    owe(gx.at[0, 0, pl.ds(0, 4)], sa.at[0])
-    owe(gx.at[0, 0, pl.ds(0, 3)], sa.at[0])
-    owe(gy.at[0, 0, pl.ds(0, 4)], sa.at[1])
-    owe(gy.at[0, 0, pl.ds(0, 3)], sa.at[1])
+    owe(gx.at[pl.ds(0, 5), 0, 0], sa.at[0])
+    owe(gy.at[pl.ds(0, 5), 0, 0], sa.at[1])
 
     def across_second(q):
         take(gx.at[q, x, pl.ds(0, 2)], ra.at[q])
@@ -287,8 +312,6 @@
             push(gy.at[q, y, x], gy.at[q, y, x], sb.at[1], rby.at[q], dev(xp(k), y, z, c))
 
     def across_third(q):
-        if 0 < q <= SLANTED:
-            take(gx.at[q, x, pl.ds(0, 2)], ra.at[q])
         take(gx.at[q, x, pl.ds(0, 3)], rbx.at[q])
         for k in SPREAD:
             push(gx.at[q, x], gx.at[q, x], sc.at[0], rcx.at[q], dev(xp(k), y, z, c))
@@ -296,57 +319,51 @@
         for k in SPREAD:
             push(gy.at[q, y], gy.at[q, y], sc.at[1], rcy.at[q], dev(x, yp(k), z, c))
 
+    def plane_to_next():
+        take(gx.at[0, pl.ds(0, 3)], rcx.at[0])
+        take(gy.at[0, pl.ds(0, 3)], rcy.at[0])
+        for q in (1, 2):
+            to = dev(x, y, zp(NZ - near[q]), c)
+            push(gx.at[0], gx.at[q], sc.at[2], rbx.at[q], to)
+            push(gy.at[0], gy.at[q], sc.at[3], rby.at[q], to)
+
     def last_phase(q, acc):
-        take(gx.at[q, pl.ds(0, 3)], rcx.at[q])
-        take(gy.at[q, pl.ds(0, 3)], rcy.at[q])
+        if q in (1, 2):
+            take(gx.at[q], rbx.at[q])
+            take(gy.at[q], rby.at[q])
+        elif q > 2:
+            take(gx.at[q, pl.ds(0, 3)], rcx.at[q])
+            take(gy.at[q, pl.ds(0, 3)], rcy.at[q])
         for py in range(NY):
             right = jnp.concatenate(
                 [jnp.concatenate([gx[q, px, py], gy[q, py, px]], axis=0) for px in range(NX)], axis=1
             )
-            acc = acc + lax.dot_general(adj[NZ - 1 - q, py], right, across, preferred_element_type=F32)
+            acc = acc + lax.dot_general(adj[STEPS.index(near[q]), py], right, across, preferred_element_type=F32)
         return acc
 
     def weights_second():
-        take(rw1, rw.at[0])
-        for share, own in ((0, x), (1, y)):
-            part = w0[share, own]
-            for k in range(3):
-                part = part + rw1[3 * share + k]
-            w1[share] = part.reshape(4, 8, B)
-        for k in SPREAD:
-            push(w1.at[0, yp(k)], rw2.at[k - 1], sw.at[1], rw.at[1], dev(x, yp(k), z, c))
-            push(w1.at[1, xp(k)], rw2.at[k + 2], sw.at[1], rw.at[1], dev(xp(k), y, z, c))
-        owe(rw2, sw.at[1])
+        rw1[here] = w0[here]
+        take(rw1.at[pl.ds(0, 15)], rw.at[0])
+        total = rw1[0]
+        for k in range(1, 16):
+            total = total + rw1[k]
+        rw3[z] = total
+        for k in range(1, NZ):
+            push(rw3.at[z], rw3.at[z], sw.at[1], rw.at[1], dev(x, y, zp(k), c))
+        owe(rw3.at[pl.ds(0, 7)], sw.at[1])
 
     def weights_third():
-        take(rw2, rw.at[1])
-        rw3[z, 0] = w1[0, y] + rw2[0] + rw2[1] + rw2[2]
-        rw3[z, 1] = w1[1, x] + rw2[3] + rw2[4] + rw2[5]
-        for k in range(1, NZ):
-            push(rw3.at[z], rw3.at[z], sw.at[2], rw.at[2], dev(x, y, zp(k), c))
-        owe(rw3.at[pl.ds(0, 7)], sw.at[2])
-
-    def weights_fourth():
-        take(rw3.at[pl.ds(0, 7)], rw.at[2])
+        take(rw3.at[pl.ds(0, 7)], rw.at[1])
         total = rw3[0]
         for k in range(1, NZ):
             total = total + rw3[k]
-        wg[0, x, y] = total[0]
-        wg[1, y, x] = total[1]
-        for k in SPREAD:
-            push(wg.at[0, x, y], wg.at[0, x, y], sw.at[3], rw.at[3], dev(x, yp(k), z, c))
-            push(wg.at[1, y, x], wg.at[1, y, x], sw.at[3], rw.at[3], dev(xp(k), y, z, c))
-        owe(rw2, sw.at[3])
-
-    def weights_fifth():
-        take(rw2, rw.at[3])
-        for k in SPREAD:
-            push(wg.at[0, x], wg.at[0, x], sw.at[4], rw.at[4], dev(xp(k), y, z, c))
-            push(wg.at[1, y], wg.at[1, y], sw.at[4], rw.at[4], dev(x, yp(k), z, c))
-        owe(rw1, sw.at[4])
+        wg[here] = total
+        for i, j in plane:
+            push(wg.at[here], wg.at[here], sw.at[2], rw.at[2], dev(xp(i), yp(j), z, c))
+        owe(rw1.at[pl.ds(0, 15)], sw.at[2])
 
     acc = jnp.zeros((B, 64), F32)
-    weights = {2: weights_second, 3: weights_third, 4: weights_fourth, 5: weights_fifth}
+    weights = {2: weights_second, 3: weights_third}
     for step in PLAN:
         what, q = step[0], int(step[1])
         if what == "s":
@@ -355,20 +372,24 @@
             across_third(q)
         elif what == "w":
             weights[q]()
+        elif what == "r":
+            plane_to_next()
         else:
             acc = last_phase(q, acc)
-    owe(gx.at[:, 0, pl.ds(0, 3)], sb.at[0])
-    owe(gy.at[:, 0, pl.ds(0, 3)], sb.at[1])
-    owe(gx.at[:, pl.ds(0, 3)], sc.at[0])
-    owe(gy.at[:, pl.ds(0, 3)], sc.at[1])
+    owe(gx.at[pl.ds(0, 6), 0, pl.ds(0, 3)], sb.at[0])
+    owe(gy.at[pl.ds(0, 6), 0, pl.ds(0, 3)], sb.at[1])
+    owe(gx.at[pl.ds(0, 6), pl.ds(0, 3)], sc.at[0])
+    owe(gy.at[pl.ds(0, 6), pl.ds(0, 3)], sc.at[1])
+    owe(gx.at[pl.ds(0, 2)], sc.at[2])
+    owe(gy.at[pl.ds(0, 2)], sc.at[3])
 
     none = jnp.zeros((B, 64), F32)
     placed = jnp.where(c == 0, jnp.concatenate([acc, none], axis=1), jnp.concatenate([none, acc], axis=1))
     gis[...] = placed + direct
     push(gis, gir, sg.at[1], rsg.at[1], dev(x, y, z, oc))
-    take(rw1, rw.at[4])
-    emit.append(pltpu.make_async_copy(wg.at[0], gs_h, out_sem.at[1]))
-    emit.append(pltpu.make_async_copy(wg.at[1], gn_h, out_sem.at[2]))
+    take(rw1.at[pl.ds(0, 15)], rw.at[2])
+    emit.append(pltpu.make_async_copy(wg.at[:, pl.ds(0, 8)], gs_h, out_sem.at[1]))
+    emit.append(pltpu.make_async_copy(wg.at[:, pl.ds(8, 8)], gn_h, out_sem.at[2]))
     emit[1].start()
     emit[2].start()
 
@@ -404,8 +425,8 @@
         out_shape=(
             jax.ShapeDtypeStruct((B, B), BF),
             jax.ShapeDtypeStruct((B, B), BF),
-            jax.ShapeDtypeStruct((4, 4, 8, B), F32),
-            jax.ShapeDtypeStruct((4, 4, 8, B), F32),
+            jax.ShapeDtypeStruct((16, 8, B), F32),
+            jax.ShapeDtypeStruct((16, 8, B), F32),
         ),
         in_specs=[hbm] * 7,
         out_specs=(hbm,) * 4,
@@ -424,41 +445,42 @@
             V((NZ, 3, NX, 32, B), BF),
             V((NZ, NY, 32, B), BF),
             V((NZ, NX, 32, B), BF),
-            V((5, NY, 32, B), BF),
-            V((5, NX, 32, B), BF),
+            V((3, NY, 32, B), BF),
+            V((3, NX, 32, B), BF),
+            V((2, NX, NY, 32, B), BF),
+            V((2, NY, NX, 32, B), BF),
+            V((2, NX, 4, B), F32),
             V((2, NY, 32, B), BF),
             V((2, NX, 32, B), BF),
             V((NY, 32, B), BF),
             V((NX, 32, B), BF),
             V((16, 32, B), BF),
-            V((NX, NZ, 4, B), F32),
-            V((3, NZ, 4, B), F32),
+            V((NZ, NX, 4, B), F32),
+            V((NZ, 3, 4, B), F32),
             V((NZ, 4, B), F32),
-            V((NZ - 1, 4, B), F32),
+            V((5, 4, B), F32),
             V((4, B), F32),
             V((3, 4, B), F32),
             V((B, B), F32),
             V((64, B), F32),
             V((NZ, NX, NY, 32, B), BF),
             V((NZ, NY, NX, 32, B), BF),
-            V((2, 4, 32, B), F32),
-            V((6, 32, B), F32),
-            V((2, 4, 8, B), F32),
-            V((6, 8, B), F32),
-            V((NZ, 2, 8, B), F32),
-            V((2, 4, 4, 8, B), F32),
+            V((16, 16, B), F32),
+            V((16, 16, B), F32),
+            V((NZ, 16, B), F32),
+            V((16, 16, B), F32),
             V((B, B), F32),
             V((B, B), F32),
             dma((11,)),
-            dma((2,)), dma((NZ,)), dma((NZ,)),
+            dma((5,)), dma((3,)), dma((NZ,)), dma((NZ,)),
             dma((2,)), dma((2,)), dma((2, 2)),
             dma(()), dma(()),
-            dma((3,)), dma((3,)),
+            dma((3,)), dma((3,)), dma((NZ,)),
             dma((2,)), dma((2,)),
             dma((2,)), dma((NZ,)),
             dma((2,)), dma((NZ,)), dma((NZ,)),
-            dma((2,)), dma((NZ,)), dma((NZ,)),
-            dma((5,)), dma((5,)),
+            dma((4,)), dma((NZ,)), dma((NZ,)),
+            dma((3,)), dma((3,)),
             dma((4,)),
             pltpu.SemaphoreType.REGULAR,
         ],

time: 61 us -> 57.1 us (0.936)
  Pallas kernels: 60.2 us -> 56.3 us
    pallas_call x1, Pallas kernels: 58.6 us -> 54.7 us  [on_device(): pl.pallas_call(kernel, out_shape=(jax.ShapeDtypeStruct((B, B), BF), jax.S...]
where the time goes in v4:
time: 57.1 us; the launch traced here: 56.9 us
  Pallas kernels  56.3 us (99%)
  between operations  0.64 us (1%)
    pallas_call x1, Pallas kernels, on_device(): pl.pallas_call(kernel, out_shape=(jax.ShapeDtypeStruct((B, B), BF), jax.S...  54.7 us
    pallas_call x1, Pallas kernels, on_device(): pl.pallas_call(hand_out, out_shape=tuple((jax.ShapeDtypeStruct(r.shape, r...  1.61 us

profile of v4, /device:TPU:1, one launch (start us, length us, event | category | flops | bytes accessed | tf_op | source)
XLA Modules:
  0.0 56.9 jit_solution(7172500606028690285)
XLA Ops:
  0.6 54.7 %sage.1 = (bf16[128,128]{1,0:T(8,128)(2,1)}, bf16[128,128]{1,0:T(8,128)(2,1)}, f32[16,8,128]{2,1,0:T(8,128)}, f32[16,8,128]{2,1,0:T(8,128)}) custom-call(bf16[128,128]{1,0:T(8,128)(2,1)} %feat_h.1, bf16[128,128]{1,0:T(8,128)(2,1)} %ws_h.1, bf16[128,128]{1,0:T(8,128)(2,1)} %wn_h.1, bf16[128,128,128]{2,1,0:T(8,128)(2,1)} %tiles_h.1, s32[1,128]{1,0:T(1,128)} %bitcast.4, ...), custom_call_target="tpu_custom_call" | custom-call | tf_op jit(solution)/shard_map/sage/pallas_call | solution.py:423
  55.3 1.6 %hand_out.1 = (bf16[128,128]{1,0:T(8,128)(2,1)}, bf16[128,128]{1,0:T(8,128)(2,1)}, f32[16,8,128]{2,1,0:T(8,128)}, f32[16,8,128]{2,1,0:T(8,128)}) custom-call(bf16[128,128]{1,0:T(8,128)(2,1)} %get-tuple-element.12.refs_0_, bf16[128,128]{1,0:T(8,128)(2,1)} %get-tuple-element.13.refs_1_, f32[16,8,128]{2,1,0:T(8,128)} %get-tuple-element.14.refs_2_, ...), custom_call_target="tpu_custom_call" | custom-call | tf_op jit(solution)/shard_map/hand_out/pallas_call | solution.py:492

commit v5 on v4

--- a/solution.py
+++ b/solution.py
@@ -11,7 +11,7 @@
 NX, NY, NZ = 4, 4, 8
 B = 128
 SPREAD = (2, 1, 3)
-PLAN = ('s3', 's4', 't0', 's5', 's6', 'w2', 's7', 't3', 't4', 'r0', 't5', 't6', 'l0', 'w3', 't7', 'l3', 'l4', 'l5', 'l6', 'l1', 'l2', 'l7')
+PLAN = ('s3', 's4', 't0', 's5', 's6', 'w2', 's7', 't3', 't4', 'r0', 't5', 't6', 't7', 'l0', 'w3', 'l3', 'l4', 'l5', 'l6', 'l1', 'l2', 'l7')
 
 
 STEPS = (1, 7, 3, 5, 4, 2, 6, 0)
@@ -21,13 +21,13 @@
 
 def kernel(
     feat_h, ws_h, wn_h, tiles_h, dest_h, outside_h, cot_h,
-    out_h, gi_h, gs_h, gn_h,
-    feat, ws, wn, dest, outside, cot, out_o, gi_o,
-    tiles, adj, xt, idx_v, idx_s, selfp,
+    out_h, gis_h, gir_h, gs_h, gn_h,
+    feat, ws, wn, dest, outside, cot, out_o,
+    tiles, adj, xt, idx_v, idx_s, selfp, wnt, cott,
     sx, sy, r1x, r1y, p1x, p1y, r2x, r2y, rawx, rawy, rawl, rpx, rpy, p2x, p2y, r3,
     lk, rlk1, plk, rlk2, lk2, rlk3,
     gpart, grecv, gx, gy,
-    w0, rw1, rw3, wg, gis, gir,
+    w0, rw1, rw3, wg, gis,
     load_sem, s1, rraw, rs1x, rs1y, s2, rs2, rsp, s3, rs3, sl, rsl, rsl1, sg, rsg,
     sa, ra, sb, rbx, rby, sc, rcx, rcy, sw, rw, out_sem, past,
 ):
@@ -106,8 +106,6 @@
     xt[0:B, :] = features.astype(F32).T.astype(BF)
     xh = xt[pl.ds(pl.multiple_of(c * 64, 64), 64), :]
     left = jnp.concatenate([xh, jnp.ones((16, B), BF)], axis=0)
-    loads[2].wait()
-    selfp[...] = jnp.dot(features, ws[...], preferred_element_type=F32)
     table.wait()
     for load in loads[6:]:
         load.wait()
@@ -139,7 +137,7 @@
             push(lk.at[p, xp(k) + c * (yp(k) - xp(k))], rlk1.at[p, k - 1], sl.at[0], rsl1.at[p], to)
 
     def to_next(p, code):
-        dz = lax.rem(code, 8)
+        dz = code % 8
         partial_sums(p, dz)
         to = dev(x, y, zp(dz), c)
         push(sx.at[p], rawx.at[p], s1.at[2], rraw.at[0], to)
@@ -148,13 +146,20 @@
         return code // 8
 
     def to_far(p, code):
-        partial_sums(p, lax.rem(code, 8))
+        partial_sums(p, code % 8)
         send_first(p)
         return code // 8
 
+    to_far(2, PACKED // 64)
     lax.fori_loop(0, 2, to_next, PACKED)
-    lax.fori_loop(2, OWN, to_far, PACKED // 64)
+    lax.fori_loop(3, OWN, to_far, PACKED // 512)
     partial_sums(OWN, 0)
+
+    for load in loads[2:5]:
+        load.wait()
+    wnt[...] = wn[...].astype(F32).T.astype(BF)
+    cott[...] = cot[...].astype(F32).T
+    selfp[...] = jnp.dot(ws[...].astype(F32).T.astype(BF), xt[...], preferred_element_type=F32)
 
     def send_own():
         for sent, raw, i in ((sx, rawx, 0), (sy, rawy, 1)):
@@ -267,18 +272,14 @@
     mean_t = jnp.concatenate(pieces, axis=0) * inverse
     mean_tb = mean_t.astype(BF)
 
-    loads[3].wait()
-    loads[4].wait()
-    pre = selfp[...] + jnp.dot(mean_t.T.astype(BF), wn[...], preferred_element_type=F32)
+    pre = selfp[...] + jnp.dot(wnt[...], mean_tb, preferred_element_type=F32)
     sigma = jax.nn.sigmoid(pre)
-    out_o[...] = (pre * sigma).astype(BF)
-    emit = [pltpu.make_async_copy(out_o, out_h, out_sem.at[0])]
-    emit[0].start()
-    dpre = (cot[...].astype(F32) * sigma * (1.0 + pre * (1.0 - sigma))).astype(BF)
+    dpre_t = (cott[...] * sigma * (1.0 + pre * (1.0 - sigma))).astype(BF)
     across = (((1,), (1,)), ((), ()))
-    gpart[...] = lax.dot_general(wn[...], dpre, across, preferred_element_type=F32) * inverse
+    gpart[...] = jnp.dot(wn[...], dpre_t, preferred_element_type=F32) * inverse
     push(gpart.at[pl.ds(pl.multiple_of(oc * 64, 64), 64)], grecv, sg.at[0], rsg.at[0], dev(x, y, z, oc))
     owe(grecv, sg.at[0])
+    dpre = dpre_t.astype(F32).T.astype(BF)
     grad_s = jnp.dot(xt[...], dpre, preferred_element_type=F32)
     grad_n = jnp.dot(mean_tb, dpre, preferred_element_type=F32)
     w0[:, 0:8, :] = grad_s.reshape(16, 8, B)
@@ -289,6 +290,9 @@
         push(w0.at[xp(i) * NY + yp(j)], rw1.at[here], sw.at[0], rw.at[0], dev(xp(i), yp(j), z, c))
     owe(rw1.at[pl.ds(0, 15)], sw.at[0])
     direct = lax.dot_general(dpre, ws[...], across, preferred_element_type=F32)
+    out_o[...] = (pre * sigma).T.astype(BF)
+    emit = [pltpu.make_async_copy(out_o, out_h, out_sem.at[0])]
+    emit[0].start()
     take(grecv, rsg.at[0])
     gfull = (gpart[pl.ds(pl.multiple_of(c * 64, 64), 64), :] + grecv[...]).astype(BF)
     gx[0, x, y] = gfull[0:32]
@@ -386,30 +390,38 @@
     none = jnp.zeros((B, 64), F32)
     placed = jnp.where(c == 0, jnp.concatenate([acc, none], axis=1), jnp.concatenate([none, acc], axis=1))
     gis[...] = placed + direct
-    push(gis, gir, sg.at[1], rsg.at[1], dev(x, y, z, oc))
+    push(gis, gir_h, sg.at[1], rsg.at[1], dev(x, y, z, oc))
+    emit.append(pltpu.make_async_copy(gis, gis_h, out_sem.at[3]))
+    emit[1].start()
     take(rw1.at[pl.ds(0, 15)], rw.at[2])
     emit.append(pltpu.make_async_copy(wg.at[:, pl.ds(0, 8)], gs_h, out_sem.at[1]))
     emit.append(pltpu.make_async_copy(wg.at[:, pl.ds(8, 8)], gn_h, out_sem.at[2]))
-    emit[1].start()
     emit[2].start()
+    emit[3].start()
 
     settle()
-    take(gir, rsg.at[1])
-    gi_o[...] = (gis[...] + gir[...]).astype(BF)
-    emit.append(pltpu.make_async_copy(gi_o, gi_h, out_sem.at[3]))
-    emit[3].start()
+    take(gis, rsg.at[1])
     take(gis, sg.at[1])
     for copy in emit:
         copy.wait()
 
 
-def hand_out(*refs):
-    sources, targets, held, sems = refs[0:4], refs[4:8], refs[8:12], refs[12]
-    inward = [pltpu.make_async_copy(a, b, sems.at[0, i]) for i, (a, b) in enumerate(zip(sources, held))]
-    outward = [pltpu.make_async_copy(a, b, sems.at[1, i]) for i, (a, b) in enumerate(zip(held, targets))]
+def hand_out(out_h, gis_h, gir_h, gs_h, gn_h, out_t, gi_t, gs_t, gn_t, out, gis, gir, gs, gn, gi, sems):
+    inward = [
+        pltpu.make_async_copy(a, b, sems.at[0, i])
+        for i, (a, b) in enumerate(((gis_h, gis), (gir_h, gir), (out_h, out), (gs_h, gs), (gn_h, gn)))
+    ]
+    outward = [
+        pltpu.make_async_copy(a, b, sems.at[1, i])
+        for i, (a, b) in enumerate(((gi, gi_t), (out, out_t), (gs, gs_t), (gn, gn_t)))
+    ]
     for copy in inward:
         copy.start()
-    for first, second in zip(inward, outward):
+    inward[0].wait()
+    inward[1].wait()
+    gi[...] = (gis[...] + gir[...]).astype(BF)
+    outward[0].start()
+    for first, second in zip(inward[2:], outward[1:]):
         first.wait()
         second.start()
     for copy in outward:
@@ -424,20 +436,23 @@
         kernel,
         out_shape=(
             jax.ShapeDtypeStruct((B, B), BF),
-            jax.ShapeDtypeStruct((B, B), BF),
+            jax.ShapeDtypeStruct((B, B), F32),
+            jax.ShapeDtypeStruct((B, B), F32),
             jax.ShapeDtypeStruct((16, 8, B), F32),
             jax.ShapeDtypeStruct((16, 8, B), F32),
         ),
         in_specs=[hbm] * 7,
-        out_specs=(hbm,) * 4,
+        out_specs=(hbm,) * 5,
         scratch_shapes=[
             V((B, B), BF), V((B, B), BF), V((B, B), BF), V((1, B), jnp.int32), V((1, B), jnp.int32),
-            V((B, B), BF), V((B, B), BF), V((B, B), BF),
+            V((B, B), BF), V((B, B), BF),
             V((B + 1, B, B), BF),
             V((NZ, NY, B, NX * B), BF),
             V((B, B), BF),
             V((8, B), jnp.int32),
             pltpu.SMEM((8, B), jnp.int32),
+            V((B, B), F32),
+            V((B, B), BF),
             V((B, B), F32),
             V((NZ, NX, NY, 32, B), BF),
             V((NZ, NY, NX, 32, B), BF),
@@ -470,7 +485,6 @@
             V((NZ, 16, B), F32),
             V((16, 16, B), F32),
             V((B, B), F32),
-            V((B, B), F32),
             dma((11,)),
             dma((5,)), dma((3,)), dma((NZ,)), dma((NZ,)),
             dma((2,)), dma((2,)), dma((2, 2)),
@@ -491,10 +505,10 @@
     )(features, w_self, w_neigh, tiles, dest.reshape(1, B), outside.reshape(1, B), cotangent)
     results = pl.pallas_call(
         hand_out,
-        out_shape=tuple(jax.ShapeDtypeStruct(r.shape, r.dtype) for r in results),
-        in_specs=[hbm] * 4,
+        out_shape=tuple(jax.ShapeDtypeStruct(r.shape, t) for r, t in zip((results[0],) + results[2:], (BF, BF, F32, F32))),
+        in_specs=[hbm] * 5,
         out_specs=(hbm,) * 4,
-        scratch_shapes=[V(r.shape, r.dtype) for r in results] + [dma((2, 4))],
+        scratch_shapes=[V(r.shape, r.dtype) for r in results] + [V((B, B), BF), dma((2, 5))],
         compiler_params=pltpu.CompilerParams(vmem_limit_bytes=60 * 2**20),
         name="hand_out",
     )(*results)

time: 57.1 us -> 55.1 us (0.965)
  Pallas kernels: 56.3 us -> 54.3 us
    pallas_call x1, Pallas kernels: 54.7 us -> 52.6 us  [on_device(): pl.pallas_call(kernel, out_shape=(jax.ShapeDtypeStruct((B, B), BF), jax.S...]
where the time goes in v5:
time: 55.1 us; the launch traced here: 54.9 us
  Pallas kernels  54.3 us (99%)
  between operations  0.64 us (1%)
    pallas_call x1, Pallas kernels, on_device(): pl.pallas_call(kernel, out_shape=(jax.ShapeDtypeStruct((B, B), BF), jax.S...  52.6 us
    pallas_call x1, Pallas kernels, on_device(): pl.pallas_call(hand_out, out_shape=tuple((jax.ShapeDtypeStruct(r.shape, t...  1.67 us

profile of v5, /device:TPU:1, one launch (start us, length us, event | category | flops | bytes accessed | tf_op | source)
XLA Modules:
  0.0 54.9 jit_solution(4712388211211102006)
XLA Ops:
  0.6 52.6 %sage.1 = (bf16[128,128]{1,0:T(8,128)(2,1)}, f32[128,128]{1,0:T(8,128)}, f32[128,128]{1,0:T(8,128)}, f32[16,8,128]{2,1,0:T(8,128)}, f32[16,8,128]{2,1,0:T(8,128)}) custom-call(bf16[128,128]{1,0:T(8,128)(2,1)} %feat_h.1, bf16[128,128]{1,0:T(8,128)(2,1)} %ws_h.1, bf16[128,128]{1,0:T(8,128)(2,1)} %wn_h.1, bf16[128,128,128]{2,1,0:T(8,128)(2,1)} %tiles_h.1, ...), custom_call_target="tpu_custom_call" | custom-call | tf_op jit(solution)/shard_map/sage/pallas_call | solution.py:435
  53.3 1.7 %hand_out.1 = (bf16[128,128]{1,0:T(8,128)(2,1)}, bf16[128,128]{1,0:T(8,128)(2,1)}, f32[16,8,128]{2,1,0:T(8,128)}, f32[16,8,128]{2,1,0:T(8,128)}) custom-call(bf16[128,128]{1,0:T(8,128)(2,1)} %get-tuple-element.13.out_h, f32[128,128]{1,0:T(8,128)} %get-tuple-element.14.gis_h, f32[128,128]{1,0:T(8,128)} %get-tuple-element.15.gir_h, ...), custom_call_target="tpu_custom_call" | custom-call | tf_op jit(solution)/shard_map/hand_out/pallas_call | solution.py:506

commit v6 on v5

--- a/solution.py
+++ b/solution.py
@@ -22,11 +22,11 @@
 def kernel(
     feat_h, ws_h, wn_h, tiles_h, dest_h, outside_h, cot_h,
     out_h, gis_h, gir_h, gs_h, gn_h,
-    feat, ws, wn, dest, outside, cot, out_o,
+    feat, ws, wn, dest, outside, cot, out_o, ws2, wn2, cot2,
     tiles, adj, xt, idx_v, idx_s, selfp, wnt, cott,
     sx, sy, r1x, r1y, p1x, p1y, r2x, r2y, rawx, rawy, rawl, rpx, rpy, p2x, p2y, r3,
     lk, rlk1, plk, rlk2, lk2, rlk3,
-    gpart, grecv, gx, gy,
+    gx, gy,
     w0, rw1, rw3, wg, gis,
     load_sem, s1, rraw, rs1x, rs1y, s2, rs2, rsp, s3, rs3, sl, rsl, rsl1, sg, rsg,
     sa, ra, sb, rbx, rby, sc, rcx, rcy, sw, rw, out_sem, past,
@@ -112,6 +112,12 @@
     pl.semaphore_wait(barrier, len(line))
     pl.semaphore_signal(past, inc=1, device_id=dev(x, y, z, oc), device_id_type=MESH)
 
+    for load in loads[2:5]:
+        load.wait()
+    for i, (mine, other) in enumerate(((ws, ws2), (wn, wn2), (cot, cot2))):
+        push(mine, other, sg.at[i + 2], rsg.at[i], dev(x, y, z, oc))
+        owe(mine, sg.at[i + 2])
+
     def partial_sums(p, dz):
         to_z = zp(dz)
         for py in range(NY):
@@ -155,11 +161,12 @@
     lax.fori_loop(3, OWN, to_far, PACKED // 512)
     partial_sums(OWN, 0)
 
-    for load in loads[2:5]:
-        load.wait()
-    wnt[...] = wn[...].astype(F32).T.astype(BF)
-    cott[...] = cot[...].astype(F32).T
-    selfp[...] = jnp.dot(ws[...].astype(F32).T.astype(BF), xt[...], preferred_element_type=F32)
+    def transposed(i, w_self, w_neigh, gradient):
+        wnt[i] = w_neigh[...].astype(F32).T.astype(BF)
+        cott[i] = gradient[...].astype(F32).T
+        selfp[i] = jnp.dot(w_self[...].astype(F32).T.astype(BF), xt[...], preferred_element_type=F32)
+
+    transposed(0, ws, wn, cot)
 
     def send_own():
         for sent, raw, i in ((sx, rawx, 0), (sy, rawy, 1)):
@@ -206,8 +213,12 @@
         second_phase(p)
         sum_links(p)
         push(plk.at[p], rlk2.at[p - 2], sl.at[1], rsl.at[1], dev(x, y, zp(STEPS[p]), c))
-        if p == 3:
+        if p == 4:
             send_own()
+        if p == 4:
+            for i, other in enumerate((ws2, wn2, cot2)):
+                take(other, rsg.at[i])
+            transposed(1, ws2, wn2, cot2)
     owe(sx.at[pl.ds(2, 6), pl.ds(0, 3)], s1.at[0])
     owe(sy.at[pl.ds(2, 6), pl.ds(0, 3)], s1.at[1])
     owe(rawx, s1.at[2])
@@ -272,13 +283,32 @@
     mean_t = jnp.concatenate(pieces, axis=0) * inverse
     mean_tb = mean_t.astype(BF)
 
-    pre = selfp[...] + jnp.dot(wnt[...], mean_tb, preferred_element_type=F32)
-    sigma = jax.nn.sigmoid(pre)
-    dpre_t = (cott[...] * sigma * (1.0 + pre * (1.0 - sigma))).astype(BF)
+    def layer(i):
+        pre = selfp[i] + jnp.dot(wnt[i], mean_tb, preferred_element_type=F32)
+        sigma = jax.nn.sigmoid(pre)
+        return pre * sigma, (cott[i] * sigma * (1.0 + pre * (1.0 - sigma))).astype(BF)
+
     across = (((1,), (1,)), ((), ()))
-    gpart[...] = jnp.dot(wn[...], dpre_t, preferred_element_type=F32) * inverse
-    push(gpart.at[pl.ds(pl.multiple_of(oc * 64, 64), 64)], grecv, sg.at[0], rsg.at[0], dev(x, y, z, oc))
-    owe(grecv, sg.at[0])
+    half = pl.ds(pl.multiple_of(c * 64, 64), 64)
+    result, dpre_t = layer(0)
+    _, other_t = layer(1)
+    gfull = jnp.dot(wn[half, :], dpre_t, preferred_element_type=F32)
+    gfull = gfull + jnp.dot(wn2[half, :], other_t, preferred_element_type=F32)
+    gfull = (gfull * inverse).astype(BF)
+    gx[0, x, y] = gfull[0:32]
+    gy[0, y, x] = gfull[32:64]
+
+    near = (0, 7, 1, 6, 2, 5, 3, 4)
+    for k in SPREAD:
+        push(gx.at[0, x, y], gx.at[0, x, y], sb.at[0], rbx.at[0], dev(x, yp(k), z, c))
+        push(gy.at[0, y, x], gy.at[0, y, x], sb.at[1], rby.at[0], dev(xp(k), y, z, c))
+    for q in range(3, NZ):
+        to = dev(x, y, zp(NZ - near[q]), c)
+        push(gx.at[0, x, y], gx.at[q, x, y], sa.at[0], ra.at[q], to)
+        push(gy.at[0, y, x], gy.at[q, y, x], sa.at[1], ra.at[q], to)
+    owe(gx.at[pl.ds(0, 5), 0, 0], sa.at[0])
+    owe(gy.at[pl.ds(0, 5), 0, 0], sa.at[1])
+
     dpre = dpre_t.astype(F32).T.astype(BF)
     grad_s = jnp.dot(xt[...], dpre, preferred_element_type=F32)
     grad_n = jnp.dot(mean_tb, dpre, preferred_element_type=F32)
@@ -290,24 +320,9 @@
         push(w0.at[xp(i) * NY + yp(j)], rw1.at[here], sw.at[0], rw.at[0], dev(xp(i), yp(j), z, c))
     owe(rw1.at[pl.ds(0, 15)], sw.at[0])
     direct = lax.dot_general(dpre, ws[...], across, preferred_element_type=F32)
-    out_o[...] = (pre * sigma).T.astype(BF)
+    out_o[...] = result.T.astype(BF)
     emit = [pltpu.make_async_copy(out_o, out_h, out_sem.at[0])]
     emit[0].start()
-    take(grecv, rsg.at[0])
-    gfull = (gpart[pl.ds(pl.multiple_of(c * 64, 64), 64), :] + grecv[...]).astype(BF)
-    gx[0, x, y] = gfull[0:32]
-    gy[0, y, x] = gfull[32:64]
-
-    near = (0, 7, 1, 6, 2, 5, 3, 4)
-    for k in SPREAD:
-        push(gx.at[0, x, y], gx.at[0, x, y], sb.at[0], rbx.at[0], dev(x, yp(k), z, c))
-        push(gy.at[0, y, x], gy.at[0, y, x], sb.at[1], rby.at[0], dev(xp(k), y, z, c))
-    for q in range(3, NZ):
-        to = dev(x, y, zp(NZ - near[q]), c)
-        push(gx.at[0, x, y], gx.at[q, x, y], sa.at[0], ra.at[q], to)
-        push(gy.at[0, y, x], gy.at[q, y, x], sa.at[1], ra.at[q], to)
-    owe(gx.at[pl.ds(0, 5), 0, 0], sa.at[0])
-    owe(gy.at[pl.ds(0, 5), 0, 0], sa.at[1])
 
     def across_second(q):
         take(gx.at[q, x, pl.ds(0, 2)], ra.at[q])
@@ -361,10 +376,16 @@
         total = rw3[0]
         for k in range(1, NZ):
             total = total + rw3[k]
-        wg[here] = total
+        wg[...] = total
         for i, j in plane:
-            push(wg.at[here], wg.at[here], sw.at[2], rw.at[2], dev(xp(i), yp(j), z, c))
+            to = dev(xp(i), yp(j), z, c)
+            push(wg.at[pl.ds(0, 8)], gs_h.at[here], sw.at[2], rw.at[2], to)
+            push(wg.at[pl.ds(8, 8)], gn_h.at[here], sw.at[2], rw.at[2], to)
         owe(rw1.at[pl.ds(0, 15)], sw.at[2])
+        emit.append(pltpu.make_async_copy(wg.at[pl.ds(0, 8)], gs_h.at[here], out_sem.at[1]))
+        emit.append(pltpu.make_async_copy(wg.at[pl.ds(8, 8)], gn_h.at[here], out_sem.at[2]))
+        emit[1].start()
+        emit[2].start()
 
     acc = jnp.zeros((B, 64), F32)
     weights = {2: weights_second, 3: weights_third}
@@ -390,17 +411,13 @@
     none = jnp.zeros((B, 64), F32)
     placed = jnp.where(c == 0, jnp.concatenate([acc, none], axis=1), jnp.concatenate([none, acc], axis=1))
     gis[...] = placed + direct
-    push(gis, gir_h, sg.at[1], rsg.at[1], dev(x, y, z, oc))
+    push(gis, gir_h, sg.at[1], rsg.at[3], dev(x, y, z, oc))
     emit.append(pltpu.make_async_copy(gis, gis_h, out_sem.at[3]))
-    emit[1].start()
+    emit[3].start()
     take(rw1.at[pl.ds(0, 15)], rw.at[2])
-    emit.append(pltpu.make_async_copy(wg.at[:, pl.ds(0, 8)], gs_h, out_sem.at[1]))
-    emit.append(pltpu.make_async_copy(wg.at[:, pl.ds(8, 8)], gn_h, out_sem.at[2]))
-    emit[2].start()
-    emit[3].start()
 
     settle()
-    take(gis, rsg.at[1])
+    take(gis, rsg.at[3])
     take(gis, sg.at[1])
     for copy in emit:
         copy.wait()
@@ -446,14 +463,15 @@
         scratch_shapes=[
             V((B, B), BF), V((B, B), BF), V((B, B), BF), V((1, B), jnp.int32), V((1, B), jnp.int32),
             V((B, B), BF), V((B, B), BF),
+            V((B, B), BF), V((B, B), BF), V((B, B), BF),
             V((B + 1, B, B), BF),
             V((NZ, NY, B, NX * B), BF),
             V((B, B), BF),
             V((8, B), jnp.int32),
             pltpu.SMEM((8, B), jnp.int32),
-            V((B, B), F32),
-            V((B, B), BF),
-            V((B, B), F32),
+            V((2, B, B), F32),
+            V((2, B, B), BF),
+            V((2, B, B), F32),
             V((NZ, NX, NY, 32, B), BF),
             V((NZ, NY, NX, 32, B), BF),
             V((NZ, 3, NY, 32, B), BF),
@@ -476,21 +494,19 @@
             V((5, 4, B), F32),
             V((4, B), F32),
             V((3, 4, B), F32),
-            V((B, B), F32),
-            V((64, B), F32),
             V((NZ, NX, NY, 32, B), BF),
             V((NZ, NY, NX, 32, B), BF),
             V((16, 16, B), F32),
             V((16, 16, B), F32),
             V((NZ, 16, B), F32),
-            V((16, 16, B), F32),
+            V((16, B), F32),
             V((B, B), F32),
             dma((11,)),
             dma((5,)), dma((3,)), dma((NZ,)), dma((NZ,)),
             dma((2,)), dma((2,)), dma((2, 2)),
             dma(()), dma(()),
             dma((3,)), dma((3,)), dma((NZ,)),
-            dma((2,)), dma((2,)),
+            dma((5,)), dma((4,)),
             dma((2,)), dma((NZ,)),
             dma((2,)), dma((NZ,)), dma((NZ,)),
             dma((4,)), dma((NZ,)), dma((NZ,)),

time: 55.1 us -> 53.8 us (0.976)
  Pallas kernels: 54.3 us -> 53.1 us
    pallas_call x1, Pallas kernels: 52.6 us -> 51.4 us  [on_device(): pl.pallas_call(kernel, out_shape=(jax.ShapeDtypeStruct((B, B), BF), jax.S...]
where the time goes in v6:
time: 53.8 us; the launch traced here: 53.7 us
  Pallas kernels  53.1 us (99%)
  between operations  0.64 us (1%)
    pallas_call x1, Pallas kernels, on_device(): pl.pallas_call(kernel, out_shape=(jax.ShapeDtypeStruct((B, B), BF), jax.S...  51.4 us
    pallas_call x1, Pallas kernels, on_device(): pl.pallas_call(hand_out, out_shape=tuple((jax.ShapeDtypeStruct(r.shape, t...  1.67 us

profile of v6, /device:TPU:1, one launch (start us, length us, event | category | flops | bytes accessed | tf_op | source)
XLA Modules:
  0.0 53.7 jit_solution(12878017037488138049)
XLA Ops:
  0.6 51.4 %sage.1 = (bf16[128,128]{1,0:T(8,128)(2,1)}, f32[128,128]{1,0:T(8,128)}, f32[128,128]{1,0:T(8,128)}, f32[16,8,128]{2,1,0:T(8,128)}, f32[16,8,128]{2,1,0:T(8,128)}) custom-call(bf16[128,128]{1,0:T(8,128)(2,1)} %feat_h.1, bf16[128,128]{1,0:T(8,128)(2,1)} %ws_h.1, bf16[128,128]{1,0:T(8,128)(2,1)} %wn_h.1, bf16[128,128,128]{2,1,0:T(8,128)(2,1)} %tiles_h.1, ...), custom_call_target="tpu_custom_call" | custom-call | tf_op jit(solution)/shard_map/sage/pallas_call | solution.py:452
  52.0 1.7 %hand_out.1 = (bf16[128,128]{1,0:T(8,128)(2,1)}, bf16[128,128]{1,0:T(8,128)(2,1)}, f32[16,8,128]{2,1,0:T(8,128)}, f32[16,8,128]{2,1,0:T(8,128)}) custom-call(bf16[128,128]{1,0:T(8,128)(2,1)} %get-tuple-element.13.out_h, f32[128,128]{1,0:T(8,128)} %get-tuple-element.14.gis_h, f32[128,128]{1,0:T(8,128)} %get-tuple-element.15.gir_h, ...), custom_call_target="tpu_custom_call" | custom-call | tf_op jit(solution)/shard_map/hand_out/pallas_call | solution.py:522

commit v7 on v6

--- a/solution.py
+++ b/solution.py
@@ -11,7 +11,7 @@
 NX, NY, NZ = 4, 4, 8
 B = 128
 SPREAD = (2, 1, 3)
-PLAN = ('s3', 's4', 't0', 's5', 's6', 'w2', 's7', 't3', 't4', 'r0', 't5', 't6', 't7', 'l0', 'w3', 'l3', 'l4', 'l5', 'l6', 'l1', 'l2', 'l7')
+PLAN = ('t0', 's3', 's4', 's5', 's6', 'w2', 't3', 's7', 't4', 'r0', 't5', 't6', 't7', 'l0', 'w3', 'l3', 'l4', 'l5', 'l6', 'l1', 'l2', 'l7')
 
 
 STEPS = (1, 7, 3, 5, 4, 2, 6, 0)
@@ -80,7 +80,7 @@
     for i in range(4):
         part = pl.ds(i * 32, 32)
         loads.append(pltpu.make_async_copy(tiles_h.at[part], tiles.at[part], load_sem.at[7 + i]))
-    for load in loads:
+    for load in loads[6:] + loads[:6]:
         load.start()
 
     barrier = pltpu.get_barrier_semaphore()

time: 53.8 us -> 53.7 us (level)
  no operation moved by 1% of the time
where the time goes in v7:
time: 53.7 us; the launch traced here: 53.6 us
  Pallas kernels  52.9 us (99%)
  between operations  0.64 us (1%)
    pallas_call x1, Pallas kernels, on_device(): pl.pallas_call(kernel, out_shape=(jax.ShapeDtypeStruct((B, B), BF), jax.S...  51.3 us
    pallas_call x1, Pallas kernels, on_device(): pl.pallas_call(hand_out, out_shape=tuple((jax.ShapeDtypeStruct(r.shape, t...  1.67 us

profile of v7, /device:TPU:1, one launch (start us, length us, event | category | flops | bytes accessed | tf_op | source)
XLA Modules:
  0.0 53.6 jit_solution(17216845377087992402)
XLA Ops:
  0.6 51.3 %sage.1 = (bf16[128,128]{1,0:T(8,128)(2,1)}, f32[128,128]{1,0:T(8,128)}, f32[128,128]{1,0:T(8,128)}, f32[16,8,128]{2,1,0:T(8,128)}, f32[16,8,128]{2,1,0:T(8,128)}) custom-call(bf16[128,128]{1,0:T(8,128)(2,1)} %feat_h.1, bf16[128,128]{1,0:T(8,128)(2,1)} %ws_h.1, bf16[128,128]{1,0:T(8,128)(2,1)} %wn_h.1, bf16[128,128,128]{2,1,0:T(8,128)(2,1)} %tiles_h.1, ...), custom_call_target="tpu_custom_call" | custom-call | tf_op jit(solution)/shard_map/sage/pallas_call | solution.py:452
  51.9 1.7 %hand_out.1 = (bf16[128,128]{1,0:T(8,128)(2,1)}, bf16[128,128]{1,0:T(8,128)(2,1)}, f32[16,8,128]{2,1,0:T(8,128)}, f32[16,8,128]{2,1,0:T(8,128)}) custom-call(bf16[128,128]{1,0:T(8,128)(2,1)} %get-tuple-element.13.out_h, f32[128,128]{1,0:T(8,128)} %get-tuple-element.14.gis_h, f32[128,128]{1,0:T(8,128)} %get-tuple-element.15.gir_h, ...), custom_call_target="tpu_custom_call" | custom-call | tf_op jit(solution)/shard_map/hand_out/pallas_call | solution.py:522

commit v8 on v7

--- a/solution.py
+++ b/solution.py
@@ -302,7 +302,7 @@
     for k in SPREAD:
         push(gx.at[0, x, y], gx.at[0, x, y], sb.at[0], rbx.at[0], dev(x, yp(k), z, c))
         push(gy.at[0, y, x], gy.at[0, y, x], sb.at[1], rby.at[0], dev(xp(k), y, z, c))
-    for q in range(3, NZ):
+    for q in range(NZ - 1, 2, -1):
         to = dev(x, y, zp(NZ - near[q]), c)
         push(gx.at[0, x, y], gx.at[q, x, y], sa.at[0], ra.at[q], to)
         push(gy.at[0, y, x], gy.at[q, y, x], sa.at[1], ra.at[q], to)

time: 53.7 us -> 54.5 us (1.015)
  Pallas kernels: 52.9 us -> 53.7 us
    pallas_call x1, Pallas kernels: 51.3 us -> 52.1 us  [on_device(): pl.pallas_call(kernel, out_shape=(jax.ShapeDtypeStruct((B, B), BF), jax.S...]
where the time goes in v8:
time: 54.5 us; the launch traced here: 54.4 us
  Pallas kernels  53.7 us (99%)
  between operations  0.64 us (1%)
    pallas_call x1, Pallas kernels, on_device(): pl.pallas_call(kernel, out_shape=(jax.ShapeDtypeStruct((B, B), BF), jax.S...  52.1 us
    pallas_call x1, Pallas kernels, on_device(): pl.pallas_call(hand_out, out_shape=tuple((jax.ShapeDtypeStruct(r.shape, t...  1.67 us

profile of v8, /device:TPU:1, one launch (start us, length us, event | category | flops | bytes accessed | tf_op | source)
XLA Modules:
  0.0 54.4 jit_solution(11990658827208000296)
XLA Ops:
  0.6 52.1 %sage.1 = (bf16[128,128]{1,0:T(8,128)(2,1)}, f32[128,128]{1,0:T(8,128)}, f32[128,128]{1,0:T(8,128)}, f32[16,8,128]{2,1,0:T(8,128)}, f32[16,8,128]{2,1,0:T(8,128)}) custom-call(bf16[128,128]{1,0:T(8,128)(2,1)} %feat_h.1, bf16[128,128]{1,0:T(8,128)(2,1)} %ws_h.1, bf16[128,128]{1,0:T(8,128)(2,1)} %wn_h.1, bf16[128,128,128]{2,1,0:T(8,128)(2,1)} %tiles_h.1, ...), custom_call_target="tpu_custom_call" | custom-call | tf_op jit(solution)/shard_map/sage/pallas_call | solution.py:452
  52.7 1.7 %hand_out.1 = (bf16[128,128]{1,0:T(8,128)(2,1)}, bf16[128,128]{1,0:T(8,128)(2,1)}, f32[16,8,128]{2,1,0:T(8,128)}, f32[16,8,128]{2,1,0:T(8,128)}) custom-call(bf16[128,128]{1,0:T(8,128)(2,1)} %get-tuple-element.13.out_h, f32[128,128]{1,0:T(8,128)} %get-tuple-element.14.gis_h, f32[128,128]{1,0:T(8,128)} %get-tuple-element.15.gir_h, ...), custom_call_target="tpu_custom_call" | custom-call | tf_op jit(solution)/shard_map/hand_out/pallas_call | solution.py:522
